TPU v7x, 32 devices: a whole 2x2x4 slice. The times are simulated.
32 devices in a mesh: rep: 4 (over z), tp: 8 (over y, x, core).
Axes of the slice: x: 2, y: 2, z: 4, core: 2. Of those that a mesh axis runs over, the one named last changes fastest.
Arguments:
- tokens: bfloat16 [2048, 8192], P('rep', 'tp'), may hold values from -17 to 17
- query_weight: bfloat16 [8192, 8192], P(('rep', 'tp')), may hold values from -0.0625 to 0.0625
- output_weight: bfloat16 [8192, 8192], P(('rep', 'tp')), may hold values from -0.0625 to 0.0625
- keyval_slot: bfloat16 [4, 8, 8192, 256], P('rep', 'tp'), may hold values from -0.0625 to 0.0625
- holder: int32 [8], replicated, may hold values from 0 to 3, as said below
Outputs:
- query_local: bfloat16 [8192, 8192], P(None, 'tp')
- output_local: bfloat16 [8192, 8192], P(None, 'tp')
- keyval_local: bfloat16 [8, 8192, 256], P('tp')
- attended: bfloat16 [2048, 8192], P(('rep', 'tp'))
Inputs may be any that keep to these rules, and one draw needn't show every extreme that they name: Key-value head h is held at replica holder[h] // 1 and tensor rank 1 * h + holder[h] % 1.
All inputs are finite; a program needn't handle non-finite values.
Results may differ from a plain program's by a relative error of at most 0.019.
The roundings to bfloat16 on the way count: a program that leaves them out, or rounds other values in their place, can miss the bound.
Values may be sent and summed in bfloat16 or wider, within the bound.
A program may use at most 192 MiB of HBM per device.

v0:
```python
import math

import jax
import jax.numpy as jnp
from jax import lax
from jax.sharding import PartitionSpec as P

HD = 128
KVH = 8


def broadcast(value, axis, source):
    kept = jnp.where(lax.axis_index(axis) == source, value, 0).astype(value.dtype)
    return lax.psum(kept, axis)


def partner_2(block, axis, distance):
    count = lax.axis_size(axis)
    route = []
    for low in range(count):
        high = low | 1 << distance
        if high != low and high < count:
            route += [(low, high), (high, low)]
    return lax.ppermute(block, axis, route)


def spread_rows(matrix, replicas, ranks):
    height = matrix.shape[0]
    width = matrix.shape[1] // ranks
    blocks = matrix.reshape(height, 1, ranks, width)
    blocks = jnp.broadcast_to(blocks, (height, replicas, ranks, width))
    return blocks.reshape(height, replicas * ranks, width)


def per_device(tokens, query_weight, output_weight, keyval_slot, holder):
    ranks = lax.axis_size("tp")
    replicas = lax.axis_size("rep")
    width = query_weight.shape[1] // ranks
    query_full, output_full = (
        lax.all_to_all(
            spread_rows(query_weight, replicas, ranks),
            ("rep", "tp"),
            split_axis=1,
            concat_axis=0,
            tiled=True,
        ),
        lax.all_to_all(
            spread_rows(output_weight, replicas, ranks),
            ("rep", "tp"),
            split_axis=1,
            concat_axis=0,
            tiled=True,
        ),
    )
    query_local = query_full.reshape(-1, width)
    output_local = output_full.reshape(-1, width)
    group = ranks // KVH
    my_rank = lax.axis_index("tp")
    owner = my_rank // group
    chosen = holder[owner]
    home_replica = chosen // group
    home_place = chosen % group
    my_place = my_rank % group
    spread = broadcast(keyval_slot[0, 0], "rep", home_replica)
    for level in range(group.bit_length() - 1):
        partner = partner_2(spread, "tp", level)
        holding = (my_place ^ home_place) >> level == 0
        spread = jnp.where(holding, spread, partner)
    token_count = tokens.shape[0]
    piece = lax.all_gather(tokens, "tp", axis=1, tiled=True)
    query_sum = jnp.dot(piece, query_local, preferred_element_type=jnp.float32)
    keyval_sum = jnp.dot(piece, spread, preferred_element_type=jnp.float32)
    heads_local = width // HD
    queries = query_sum.astype(jnp.bfloat16).reshape(token_count, heads_local, HD)
    keyval = keyval_sum.astype(jnp.bfloat16)
    keys = keyval[:, :HD]
    values = keyval[:, HD:]
    scale = 1.0 / math.sqrt(HD)
    scores = jnp.einsum("qhd,kd->hqk", queries, keys, preferred_element_type=jnp.float32) * scale
    row_index = lax.broadcasted_iota(jnp.int32, (token_count, token_count), 0)
    col_index = lax.broadcasted_iota(jnp.int32, (token_count, token_count), 1)
    scores = jnp.where(col_index <= row_index, scores, -1e30)
    peak = jnp.max(scores, axis=-1, keepdims=True)
    weights = jnp.exp(scores - peak)
    weights = (weights / jnp.sum(weights, axis=-1, keepdims=True)).astype(jnp.bfloat16)
    context = jnp.einsum("hqk,kd->qhd", weights, values, preferred_element_type=jnp.float32)
    context = context.astype(jnp.bfloat16).reshape(token_count, width)
    attended = lax.psum_scatter(
        lax.dot_general(
            context, output_local, (((1,), (1,)), ((), ())), preferred_element_type=jnp.float32
        ).astype(jnp.bfloat16),
        "tp",
        scatter_dimension=0,
        tiled=True,
    )
    return (
        query_local,
        output_local,
        spread.reshape(1, spread.shape[0], spread.shape[1]),
        attended,
    )


def solution(mesh):
    in_specs = (
        P("rep", "tp"),
        P(("rep", "tp"), None),
        P(("rep", "tp"), None),
        P("rep", "tp", None, None),
        P(),
    )
    out_specs = (P(None, "tp"), P(None, "tp"), P("tp", None, None), P(("rep", "tp"), None))
    return jax.shard_map(
        per_device, mesh=mesh, in_specs=in_specs, out_specs=out_specs, check_vma=False
    )
```

profile of v0, /device:TPU:0, one launch (start us, length us, event | category | flops | bytes accessed | tf_op | source)
XLA Modules:
  0.0 1045.4 jit_solution(11078060113287050226)
XLA Ops:
  8.0 2.6 copy.27
  10.6 6.2 broadcast_in_dim.29
  16.8 7.4 all-to-all-start
  24.3 4.8 copy.26
  29.1 367.9 %all-to-all-done = bf16[256,32,1024]{2,0,1:T(8,128)(2,1)} async-done(((bf16[256,32,1024]{2,0,1:T(8,128)(2,1)}), bf16[256,32,1024]{2,0,1:T(8,128)(2,1)}, u32[]{:S(2)}, u32[]{:S(2)}) %all-to-all-start) | async-done | bytes 16777248 | tf_op jit(solution)/shard_map/all_to_all | solution.py:40
  397.0 7.5 broadcast_in_dim.31
  404.4 4.0 all-to-all-start.1
  408.5 0.6 dynamic_slice.3
  409.7 2.3 select_bitcast_fusion
  412.1 0.0 all-gather.2.cloned.1.call-start
  412.1 0.5 all-gather.2.cloned.1.call-update
  412.7 0.1 iota_compare_fusion
  412.8 368.7 %all-reduce.2.cloned.1.call-done = bf16[8192,256]{1,0:T(8,128)(2,1)} async-done(((bf16[8192,256]{1,0:T(8,128)(2,1)}), bf16[8192,256]{1,0:T(8,128)(2,1)}) %all-reduce.2.cloned.1.call-update) | async-done | bytes 4194320 | tf_op jit(solution)/shard_map/psum | solution.py:14
  781.4 7.2 fusion.8
  788.6 12.6 %fusion.7 = bf16[64,8,8,128]{3,2,1,0:T(8,128)(2,1)S(1)} fusion(bf16[512,8192]{1,0:T(8,128)(2,1)S(1)} %copy-done.1, bf16[8192,1024]{1,0:T(8,128)(2,1)} %bitcast.3), kind=kOutput, calls=%fused_computation.15 | convolution fusion | flops 8590458880 | bytes 26214400 | tf_op jit(solution)/shard_map/dot_general | solution.py:71
  801.2 1.3 fusion.9
  802.5 5.6 fusion.14
  808.2 4.1 fusion.6
  812.3 97.0 %all-to-all-done.1 = bf16[256,32,1024]{2,0,1:T(8,128)(2,1)} async-done(((bf16[256,32,1024]{2,0,1:T(8,128)(2,1)}), bf16[256,32,1024]{2,0,1:T(8,128)(2,1)}, u32[]{:S(2)}, u32[]{:S(2)}) %all-to-all-start.1) | async-done | bytes 16777248 | tf_op jit(solution)/shard_map/all_to_all | solution.py:47
  909.3 29.8 %convolution_convert_fusion = bf16[512,8192]{1,0:T(8,128)(2,1)} fusion(bf16[512,1024]{0,1:T(8,128)(2,1)S(1)} %bitcast.64, bf16[8192,1024]{1,0:T(8,128)(2,1)} %bitcast.7), kind=kOutput, calls=%fused_computation.1 | convolution fusion | flops 8594128896 | bytes 26214400 | tf_op jit(solution)/shard_map/dot_general | solution.py:89
  939.1 68.8 %reduce-scatter.2.cloned.1.call-done = bf16[64,8192]{1,0:T(8,128)(2,1)} async-done(((bf16[512,8192]{1,0:T(8,128)(2,1)}), bf16[64,8192]{1,0:T(8,128)(2,1)}) %reduce-scatter.2.cloned.1.call-update) | async-done | bytes 1048592 | tf_op jit(solution)/shard_map/reduce_scatter | solution.py:88
  1007.9 13.9 %copy.31 = bf16[8192,1024]{1,0:T(8,128)(2,1)} copy(bf16[8192,1024]{1,0:T(8,128)(2,1)} %bitcast.3) | data formatting | bytes 33554432
  1021.8 14.2 %copy.32 = bf16[8192,1024]{1,0:T(8,128)(2,1)} copy(bf16[8192,1024]{1,0:T(8,128)(2,1)} %bitcast.7) | data formatting | bytes 33554432
  1035.9 2.0 copy.33
  (11 shorter events, 0.1 us)
Async XLA Ops:
  16.8 380.1 %all-to-all-start = ((bf16[256,32,1024]{2,0,1:T(8,128)(2,1)}), bf16[256,32,1024]{2,0,1:T(8,128)(2,1)}, u32[]{:S(2)}, u32[]{:S(2)}) async-start(bf16[256,32,1024]{2,0,1:T(8,128)(2,1)} %bitcast.58), calls=%async_computation | async-start | bytes 33554432 | tf_op jit(solution)/shard_map/all_to_all | solution.py:40
  404.4 4.1 copy-start.2
  404.4 504.9 %all-to-all-start.1 = ((bf16[256,32,1024]{2,0,1:T(8,128)(2,1)}), bf16[256,32,1024]{2,0,1:T(8,128)(2,1)}, u32[]{:S(2)}, u32[]{:S(2)}) async-start(bf16[256,32,1024]{2,0,1:T(8,128)(2,1)} %bitcast.57), calls=%async_computation.1 | async-start | bytes 33554432 | tf_op jit(solution)/shard_map/all_to_all | solution.py:47
  408.4 373.0 %all-reduce.2.cloned.1.call-start = ((), (), s32[]{:S(2)}) async-start(), calls=%async_computation.3 | async-start | bytes 8388608 | tf_op jit(solution)/shard_map/psum | solution.py:14
  412.1 369.4 %all-gather.2.cloned.1.call-start = ((), (), s32[]{:S(2)}) async-start(), calls=%async_computation.4 | async-start | bytes 9437184 | tf_op jit(solution)/shard_map/all_gather | solution.py:70
  412.6 595.2 %reduce-scatter.2.cloned.1.call-start = ((), (), s32[]{:S(2)}) async-start(), calls=%async_computation.5 | async-start | bytes 9437184 | tf_op jit(solution)/shard_map/reduce_scatter | solution.py:88
  781.4 7.2 copy-start.1
  1021.8 14.2 %copy-start = (bf16[8192,256]{1,0:T(8,128)(2,1)S(1)}, bf16[8192,256]{1,0:T(8,128)(2,1)}, u32[]{:S(2)}) copy-start(bf16[8192,256]{1,0:T(8,128)(2,1)} %all-reduce.2.cloned.1.call-done) | copy-start | bytes 12582916
Sparse Core Ops, SparseCore 0:
  412.2 369.1 all-reduce.1
Sparse Core Ops, SparseCore 1:
  414.6 118.2 all-gather.1
  939.2 68.7 reduce-scatter.1
where the time goes:
time: 1050 us
  waiting for transfers between devices  903 us (86%)
  matrix products  54.9 us (5%)
  local copies, waits for them, and re-layouts  51.8 us (5%)
  between operations  16.2 us (2%)
  starting transfers between devices  11.6 us (1%)
    psum x1, waiting for transfers between devices, broadcast(): return lax.psum(kept, axis)  369 us
    all_to_all x1, waiting for transfers between devices, per_device(): lax.all_to_all(spread_rows(query_weight, replicas, ranks), ('rep', 'tp'),...  368 us
    all_to_all x1, waiting for transfers between devices, per_device(): lax.all_to_all(spread_rows(output_weight, replicas, ranks), ('rep', 'tp')...  97 us
    reduce_scatter x1, waiting for transfers between devices, per_device(): lax.psum_scatter(lax.dot_general(context, output_local, (((1,), (1,)), ((...  68.8 us
    unnamed x9, local copies, waits for them, and re-layouts  30.1 us
    dot_general x1, matrix products, per_device(): lax.dot_general(context, output_local, (((1,), (1,)), ((), ())), preferre...  29.8 us
    broadcast_in_dim x4, local copies, waits for them, and re-layouts, spread_rows(): blocks = jnp.broadcast_to(blocks, (height, replicas, ranks, width))  21.1 us
  transfers between devices with their start and end apart: 5, of which 4 were waited for; matrix products, arithmetic and copies ran while one was open for 4% of the time, Pallas kernels for 0%

commit v1 on v0

v1 whole, which is shorter than its diff:
```python
import math

import jax
import jax.numpy as jnp
from jax import lax
from jax.sharding import PartitionSpec as P

HD = 128
KVH = 8
CUTS = 2


def partner_2(block, axis, distance):
    count = lax.axis_size(axis)
    route = []
    for low in range(count):
        high = low | 1 << distance
        if high != low and high < count:
            route += [(low, high), (high, low)]
    return lax.ppermute(block, axis, route)


def after(value, *earlier):
    return lax.optimization_barrier((value, *earlier))[0]


def pick(mask, value, other):
    here = lax.axis_index("rep")
    hit = here < 0
    for replica in mask:
        hit = hit | (here == replica)
    return jnp.where(hit, value, other)


def line_steps(count):
    slots = [{} for _ in range(count - 1)]
    for here in range(count):
        order = []
        for step in range(1, count):
            order += [(step, 0)] if here >= step else []
            order += [(step, 1)] if here + step < count else []
        for slot, key in enumerate(order):
            slots[slot].setdefault(key, []).append(here)
    return slots


def step_right(block, step):
    count = lax.axis_size("rep")
    return lax.ppermute(block, "rep", [(i, i + 1) for i in range(step - 1, count - 1)])


def step_left(block, step):
    count = lax.axis_size("rep")
    return lax.ppermute(block, "rep", [(i, i - 1) for i in range(1, count - step + 1)])


def slot_block(arrived, slot):
    here = lax.axis_index("rep")
    value, origin = None, None
    for (step, side), replicas in slot.items():
        got = arrived[step, side]
        start = here + step if side else here - step
        value = got if value is None else pick(replicas, got, value)
        origin = start if origin is None else pick(replicas, start, origin)
    return value, origin


def keyval_spread(own, home):
    count = lax.axis_size("rep")
    here = lax.axis_index("rep")
    held = own
    for step in range(count - 1):
        down = count - 1 - step
        pairs = [(step, step + 1), (down, down - 1)]
        routes = [pairs] if step + 1 != down - 1 else [pairs[:1], pairs[1:]]
        old = held
        for route in routes:
            got = lax.ppermute(old, "rep", route)
            take = here < 0
            if pairs[0] in route:
                take = take | ((here == step + 1) & (home <= step))
            if pairs[1] in route:
                take = take | ((here == down - 1) & (home >= down))
            held = jnp.where(take, got, held)
    return held


def per_device(tokens, query_weight, output_weight, keyval_slot, holder):
    ranks = lax.axis_size("tp")
    replicas = lax.axis_size("rep")
    here = lax.axis_index("rep")
    height, full = query_weight.shape
    width = full // ranks
    tall = height // CUTS
    slots = line_steps(replicas)

    group = ranks // KVH
    my_rank = lax.axis_index("tp")
    chosen = holder[my_rank // group]
    home_place = chosen % group
    my_place = my_rank % group

    def by_rank(matrix, cut):
        rows = matrix[cut * tall:(cut + 1) * tall].reshape(tall, ranks, width)
        rows = jnp.transpose(rows, (1, 0, 2))
        return lax.all_to_all(rows, "tp", split_axis=0, concat_axis=0, tiled=True)

    def put(whole, block, origin, cut):
        return lax.dynamic_update_slice(whole, block[None, :, None], (origin, 0, cut, 0, 0))

    spread = keyval_spread(keyval_slot[0, 0], chosen // group)
    for level in range(group.bit_length() - 1):
        partner = partner_2(spread, "tp", level)
        holding = (my_place ^ home_place) >> level == 0
        spread = jnp.where(holding, spread, partner)
    piece = lax.all_gather(tokens, "tp", axis=1, tiled=True)

    mine = {}
    last = None
    for name, matrix in (("q", query_weight), ("o", output_weight)):
        for cut in range(CUTS):
            mine[name, cut] = by_rank(matrix if last is None else after(matrix, last), cut)
            last = mine[name, cut]
    arrived = {}
    order = [(name, step, cut) for name in "qo" for step in range(1, replicas) for cut in range(CUTS)]
    gate = []
    for name, step, cut in order:
        chain = arrived.setdefault((name, cut), {})
        right = chain[step - 1, 0] if step > 1 else mine[name, cut]
        left = chain[step - 1, 1] if step > 1 else mine[name, cut]
        if len(gate) >= 2 * CUTS:
            early = gate[-2 * CUTS]
            if step == 1:
                right, left = lax.optimization_barrier((right, left, *early))[:2]
        chain[step, 0] = step_right(right, step)
        chain[step, 1] = step_left(left, step)
        gate.append((chain[step, 0], chain[step, 1]))

    def assemble(name):
        whole = jnp.zeros((replicas, ranks, CUTS, tall, width), jnp.bfloat16)
        parts = []
        for cut in range(CUTS):
            whole = put(whole, mine[name, cut], here, cut)
            parts.append((mine[name, cut], here, cut))
        for slot in slots:
            for cut in range(CUTS):
                block, origin = slot_block(arrived[name, cut], slot)
                whole = put(whole, block, origin, cut)
                parts.append((block, origin, cut))
        return whole.reshape(-1, width), parts

    query_local, _ = assemble("q")
    output_local, output_parts = assemble("o")

    token_count = tokens.shape[0]
    query_sum = jnp.dot(piece, query_local, preferred_element_type=jnp.float32)
    keyval_sum = jnp.dot(piece, spread, preferred_element_type=jnp.float32)
    heads_local = width // HD
    queries = query_sum.astype(jnp.bfloat16).reshape(token_count, heads_local, HD)
    keyval = keyval_sum.astype(jnp.bfloat16)
    keys = keyval[:, :HD]
    values = keyval[:, HD:]
    scale = 1.0 / math.sqrt(HD)
    scores = jnp.einsum("qhd,kd->hqk", queries, keys, preferred_element_type=jnp.float32) * scale
    row_index = lax.broadcasted_iota(jnp.int32, (token_count, token_count), 0)
    col_index = lax.broadcasted_iota(jnp.int32, (token_count, token_count), 1)
    scores = jnp.where(col_index <= row_index, scores, -1e30)
    peak = jnp.max(scores, axis=-1, keepdims=True)
    weights = jnp.exp(scores - peak)
    weights = (weights / jnp.sum(weights, axis=-1, keepdims=True)).astype(jnp.bfloat16)
    context = jnp.einsum("hqk,kd->qhd", weights, values, preferred_element_type=jnp.float32)
    context = context.astype(jnp.bfloat16).reshape(token_count, width)

    share = token_count // ranks
    attended = jnp.zeros((share, replicas, ranks, CUTS, tall), jnp.bfloat16)
    for block, origin, cut in output_parts:
        partial = lax.dot_general(
            context, block.reshape(-1, width), (((1,), (1,)), ((), ())),
            preferred_element_type=jnp.float32,
        ).astype(jnp.bfloat16)
        summed = lax.psum_scatter(partial, "tp", scatter_dimension=0, tiled=True)
        attended = lax.dynamic_update_slice(
            attended, summed.reshape(share, 1, ranks, 1, tall), (0, origin, 0, cut, 0)
        )
    return (
        query_local,
        output_local,
        spread.reshape(1, spread.shape[0], spread.shape[1]),
        attended.reshape(share, -1),
    )


def solution(mesh):
    in_specs = (
        P("rep", "tp"),
        P(("rep", "tp"), None),
        P(("rep", "tp"), None),
        P("rep", "tp", None, None),
        P(),
    )
    out_specs = (P(None, "tp"), P(None, "tp"), P("tp", None, None), P(("rep", "tp"), None))
    return jax.shard_map(
        per_device, mesh=mesh, in_specs=in_specs, out_specs=out_specs, check_vma=False
    )
```

time: 1050 us -> 860 us (0.82)
  waiting for transfers between devices: 903 us -> 518 us
  starting transfers between devices: 11.6 us -> 69.3 us
  other arithmetic: 8.02 us -> 60.8 us
  blocking collectives: 0 us -> 41.5 us
  local copies, waits for them, and re-layouts: 51.8 us -> 86.1 us
    ppermute x0 -> x27, waiting for transfers between devices: none -> 479 us  [the longest x12 301 us: step_left(): lax.ppermute(block, 'rep', [(i, i - 1) for i in range(1, count - step + 1)])]
    all_to_all x2 -> x3, waiting for transfers between devices: 465 us -> 38.3 us  [by_rank(): return lax.all_to_all(rows, 'tp', split_axis=0, concat_axis=0, tiled=True)]
    psum x1 -> x0, waiting for transfers between devices: 369 us -> none  [broadcast(): return lax.psum(kept, axis)]
    reduce_scatter x1 -> x8, waiting for transfers between devices: 68.8 us -> 0.15 us  [per_device(): summed = lax.psum_scatter(partial, 'tp', scatter_dimension=0, tiled=True)]
    ppermute x0 -> x27, starting transfers between devices: none -> 55.5 us  [the longest x12 28.6 us: step_right(): lax.ppermute(block, 'rep', [(i, i + 1) for i in range(step - 1, count - 1)])]
    dynamic_update_slice x0 -> x12, local copies, waits for them, and re-layouts: none -> 54.6 us  [the longest x8 42.2 us: per_device(): lax.dynamic_update_slice(attended, summed.reshape(share, 1, ranks, 1, tal...]
    dynamic_update_slice x0 -> x12, other arithmetic: none -> 46.8 us  [put(): lax.dynamic_update_slice(whole, block[None, :, None], (origin, 0, cut, 0,...]
    all_to_all x0 -> x1, blocking collectives: none -> 41.5 us  [by_rank(): return lax.all_to_all(rows, 'tp', split_axis=0, concat_axis=0, tiled=True)]
  transfers between devices with their start and end apart: 5 -> 39, of which waited for: 4 -> 15; matrix products, arithmetic and copies ran while one was open for 4% -> 23% of each run, Pallas kernels for 0% -> 0%
where the time goes in v1:
time: 860 us; the launch traced here: 851 us
  waiting for transfers between devices  518 us (60%)
  local copies, waits for them, and re-layouts  86.1 us (10%)
  starting transfers between devices  69.3 us (8%)
  other arithmetic  60.8 us (7%)
  matrix products  56.5 us (7%)
  blocking collectives  41.5 us (5%)
  between operations  18.7 us (2%)
    ppermute x12, waiting for transfers between devices, step_left(): lax.ppermute(block, 'rep', [(i, i - 1) for i in range(1, count - step + 1)])  301 us
    ppermute x12, waiting for transfers between devices, step_right(): lax.ppermute(block, 'rep', [(i, i + 1) for i in range(step - 1, count - 1)])  109 us
    ppermute x3, waiting for transfers between devices, keyval_spread(): got = lax.ppermute(old, 'rep', route)  67.7 us
    dynamic_update_slice x12, other arithmetic, put(): lax.dynamic_update_slice(whole, block[None, :, None], (origin, 0, cut, 0,...  46.8 us
    dynamic_update_slice x8, local copies, waits for them, and re-layouts, per_device(): lax.dynamic_update_slice(attended, summed.reshape(share, 1, ranks, 1, tal...  42.2 us
    all_to_all x1, blocking collectives, by_rank(): return lax.all_to_all(rows, 'tp', split_axis=0, concat_axis=0, tiled=True)  41.5 us
    all_to_all x3, waiting for transfers between devices, by_rank(): return lax.all_to_all(rows, 'tp', split_axis=0, concat_axis=0, tiled=True)  38.3 us
    ppermute x12, starting transfers between devices, step_right(): lax.ppermute(block, 'rep', [(i, i + 1) for i in range(step - 1, count - 1)])  28.6 us
  transfers between devices with their start and end apart: 39, of which 15 were waited for; matrix products, arithmetic and copies ran while one was open for 23% of the time, Pallas kernels for 0%

profile of v1, /device:TPU:0, one launch (start us, length us, event | category | flops | bytes accessed | tf_op | source)
XLA Modules:
  0.0 850.6 jit_solution(4684580100505483277)
XLA Ops:
  7.9 7.1 collective-permute-start.24
  15.3 41.5 %all_to_all.20 = bf16[8,128,1024]{2,1,0:T(8,128)(2,1)} all-to-all(bf16[8,128,1024]{2,1,0:T(8,128)(2,1)S(1)} %bitcast.167), channel_id=1, replica_groups=mesh['rep'=4,'tp'=8] {'tp'}, dimensions={0} | all-to-all | bytes 4194304 | tf_op jit(solution)/shard_map/all_to_all | solution.py:106
  70.2 38.3 %all-to-all-done.1 = bf16[8,128,1024]{2,1,0:T(8,128)(2,1)} async-done(((bf16[8,128,1024]{2,1,0:T(8,128)(2,1)}), bf16[8,128,1024]{2,1,0:T(8,128)(2,1)}, u32[]{:S(2)}, u32[]{:S(2)}) %all-to-all-start.1) | async-done | bytes 2097184 | tf_op jit(solution)/shard_map/all_to_all | solution.py:106
  127.9 21.3 %collective-permute-done = bf16[8,128,1024]{2,1,0:T(8,128)(2,1)} collective-permute-done((bf16[8,128,1024]{2,1,0:T(8,128)(2,1)}, bf16[8,128,1024]{2,1,0:T(8,128)(2,1)}, u32[]{:S(2)}, u32[]{:S(2)}) %collective-permute-start) | collective-permute-done | bytes 2097184 | tf_op jit(solution)/shard_map/ppermute | solution.py:49
  152.5 40.4 %collective-permute-done.2 = bf16[8,128,1024]{2,1,0:T(8,128)(2,1)} collective-permute-done((bf16[8,128,1024]{2,1,0:T(8,128)(2,1)}, bf16[8,128,1024]{2,1,0:T(8,128)(2,1)}, u32[]{:S(2)}, u32[]{:S(2)}) %collective-permute-start.2) | collective-permute-done | bytes 2097184 | tf_op jit(solution)/shard_map/ppermute | solution.py:49
  199.1 6.1 broadcast.9.clone
  232.4 21.3 %collective-permute-done.7 = bf16[8,128,1024]{2,1,0:T(8,128)(2,1)} collective-permute-done((bf16[8,128,1024]{2,1,0:T(8,128)(2,1)S(1)}, bf16[8,128,1024]{2,1,0:T(8,128)(2,1)}, u32[]{:S(2)}, u32[]{:S(2)}) %collective-permute-start.7) | collective-permute-done | bytes 2097184 | tf_op jit(solution)/shard_map/ppermute | solution.py:54
  265.6 80.9 %collective-permute-done.9 = bf16[8,128,1024]{2,1,0:T(8,128)(2,1)S(1)} collective-permute-done((bf16[8,128,1024]{2,1,0:T(8,128)(2,1)}, bf16[8,128,1024]{2,1,0:T(8,128)(2,1)S(1)}, u32[]{:S(2)}, u32[]{:S(2)}) %collective-permute-start.9) | collective-permute-done | bytes 2097184 | tf_op jit(solution)/shard_map/ppermute | solution.py:54
  349.8 42.8 %collective-permute-done.11 = bf16[8,128,1024]{2,1,0:T(8,128)(2,1)S(1)} collective-permute-done((bf16[8,128,1024]{2,1,0:T(8,128)(2,1)}, bf16[8,128,1024]{2,1,0:T(8,128)(2,1)S(1)}, u32[]{:S(2)}, u32[]{:S(2)}) %collective-permute-start.11) | collective-permute-done | bytes 2097184 | tf_op jit(solution)/shard_map/ppermute | solution.py:54
  395.9 17.8 %convolution_convert_fusion = bf16[1024,512]{1,0:T(8,128)(2,1)S(1)} fusion(bf16[8192,1024]{1,0:T(8,128)(2,1)} %bitcast.18, bf16[512,8192]{1,0:T(8,128)(2,1)} %all-gather.2.cloned.1.call-done), kind=kOutput, calls=%fused_computation.41 | convolution fusion | flops 8590458880 | bytes 26214400 | tf_op jit(solution)/shard_map/dot_general | solution.py:156
  413.7 67.7 %collective-permute-done.26 = bf16[8192,256]{1,0:T(8,128)(2,1)} collective-permute-done((bf16[8192,256]{1,0:T(8,128)(2,1)}, bf16[8192,256]{1,0:T(8,128)(2,1)}, u32[]{:S(2)}, u32[]{:S(2)}) %collective-permute-start.26) | collective-permute-done | bytes 4194336 | tf_op jit(solution)/shard_map/ppermute | solution.py:78
  481.4 5.5 fusion.10
  486.9 7.5 fusion.16
  510.6 5.9 collective-permute-start.14
  517.8 6.3 broadcast.9.clone.1
  530.3 20.0 %collective-permute-done.12 = bf16[8,128,1024]{2,1,0:T(8,128)(2,1)} collective-permute-done((bf16[8,128,1024]{2,1,0:T(8,128)(2,1)}, bf16[8,128,1024]{2,1,0:T(8,128)(2,1)}, u32[]{:S(2)}, u32[]{:S(2)}) %collective-permute-start.12) | collective-permute-done | bytes 2097184 | tf_op jit(solution)/shard_map/ppermute | solution.py:49
  550.3 5.7 collective-permute-done.13
  565.7 27.6 %collective-permute-done.14 = bf16[8,128,1024]{2,1,0:T(8,128)(2,1)} collective-permute-done((bf16[8,128,1024]{2,1,0:T(8,128)(2,1)}, bf16[8,128,1024]{2,1,0:T(8,128)(2,1)}, u32[]{:S(2)}, u32[]{:S(2)}) %collective-permute-start.14) | collective-permute-done | bytes 2097184 | tf_op jit(solution)/shard_map/ppermute | solution.py:49
  593.3 7.6 collective-permute-done.15
  608.9 37.1 %collective-permute-done.17 = bf16[8,128,1024]{2,1,0:T(8,128)(2,1)} collective-permute-done((bf16[8,128,1024]{2,1,0:T(8,128)(2,1)}, bf16[8,128,1024]{2,1,0:T(8,128)(2,1)}, u32[]{:S(2)}, u32[]{:S(2)}) %collective-permute-start.17) | collective-permute-done | bytes 2097184 | tf_op jit(solution)/shard_map/ppermute | solution.py:54
  656.0 34.9 %collective-permute-done.19 = bf16[8,128,1024]{2,1,0:T(8,128)(2,1)} collective-permute-done((bf16[8,128,1024]{2,1,0:T(8,128)(2,1)S(1)}, bf16[8,128,1024]{2,1,0:T(8,128)(2,1)}, u32[]{:S(2)}, u32[]{:S(2)}) %collective-permute-start.19) | collective-permute-done | bytes 2097184 | tf_op jit(solution)/shard_map/ppermute | solution.py:54
  699.7 36.1 %collective-permute-done.21 = bf16[8,128,1024]{2,1,0:T(8,128)(2,1)} collective-permute-done((bf16[8,128,1024]{2,1,0:T(8,128)(2,1)}, bf16[8,128,1024]{2,1,0:T(8,128)(2,1)}, u32[]{:S(2)}, u32[]{:S(2)}) %collective-permute-start.21) | collective-permute-done | bytes 2097184 | tf_op jit(solution)/shard_map/ppermute | solution.py:54
  743.4 35.1 %collective-permute-done.23 = bf16[8,128,1024]{2,1,0:T(8,128)(2,1)} collective-permute-done((bf16[8,128,1024]{2,1,0:T(8,128)(2,1)}, bf16[8,128,1024]{2,1,0:T(8,128)(2,1)}, u32[]{:S(2)}, u32[]{:S(2)}) %collective-permute-start.23) | collective-permute-done | bytes 2097184 | tf_op jit(solution)/shard_map/ppermute | solution.py:54
  811.5 5.3 dynamic_update_slice.91
  (135 shorter events, 212.1 us)
Async XLA Ops:
  7.2 388.8 %all-gather.2.cloned.1.call-start = ((), (), s32[]{:S(2)}) async-start(), calls=%async_computation.12 | async-start | bytes 9437184 | tf_op jit(solution)/shard_map/all_gather | solution.py:116
  7.9 106.6 %collective-permute-start.24 = (bf16[8192,256]{1,0:T(8,128)(2,1)}, bf16[8192,256]{1,0:T(8,128)(2,1)}, u32[]{:S(2)}, u32[]{:S(2)}) collective-permute-start(bf16[8192,256]{1,0:T(8,128)(2,1)} %bitcast.172), channel_id=1, source_target_pairs={{0,8},{24,16},{1,9},{25,17},{2,10},{26,18},{3,11},{27,19},{4,12},{... | collective-permute-start | bytes 12582920 | tf_op jit(solution)/shard_map/ppermute | solution.py:78
  66.2 83.0 %collective-permute-start = (bf16[8,128,1024]{2,1,0:T(8,128)(2,1)}, bf16[8,128,1024]{2,1,0:T(8,128)(2,1)}, u32[]{:S(2)}, u32[]{:S(2)}) collective-permute-start(bf16[8,128,1024]{2,1,0:T(8,128)(2,1)} %all_to_all.20), channel_id=1, source_target_pairs={{0,8},{8,16},{16,24},{1,9},{9,17},{17,25},{2,10},{10,18},{18,26},{... | collective-permute-start | bytes 6291464 | tf_op jit(solution)/shard_map/ppermute | solution.py:49
  68.9 82.4 %collective-permute-start.1 = (bf16[8,128,1024]{2,1,0:T(8,128)(2,1)}, bf16[8,128,1024]{2,1,0:T(8,128)(2,1)}, u32[]{:S(2)}, u32[]{:S(2)}) collective-permute-start(bf16[8,128,1024]{2,1,0:T(8,128)(2,1)} %all_to_all.20), channel_id=1, source_target_pairs={{8,0},{16,8},{24,16},{9,1},{17,9},{25,17},{10,2},{18,10},{26,18},{... | collective-permute-start | bytes 6291464 | tf_op jit(solution)/shard_map/ppermute | solution.py:54
  108.5 84.5 %collective-permute-start.2 = (bf16[8,128,1024]{2,1,0:T(8,128)(2,1)}, bf16[8,128,1024]{2,1,0:T(8,128)(2,1)}, u32[]{:S(2)}, u32[]{:S(2)}) collective-permute-start(bf16[8,128,1024]{2,1,0:T(8,128)(2,1)} %all-to-all-done.1), channel_id=1, source_target_pairs={{0,8},{8,16},{16,24},{1,9},{9,17},{17,25},{2,10},{10,18},{18,26},{... | collective-permute-start | bytes 6291464 | tf_op jit(solution)/shard_map/ppermute | solution.py:49
  113.2 81.8 %collective-permute-start.3 = (bf16[8,128,1024]{2,1,0:T(8,128)(2,1)}, bf16[8,128,1024]{2,1,0:T(8,128)(2,1)S(1)}, u32[]{:S(2)}, u32[]{:S(2)}) collective-permute-start(bf16[8,128,1024]{2,1,0:T(8,128)(2,1)} %all-to-all-done.1), channel_id=1, source_target_pairs={{8,0},{16,8},{24,16},{9,1},{17,9},{25,17},{10,2},{18,10},{26,18},{... | collective-permute-start | bytes 6291464 | tf_op jit(solution)/shard_map/ppermute | solution.py:54
  119.2 140.3 %collective-permute-start.25 = (bf16[8192,256]{1,0:T(8,128)(2,1)}, bf16[8192,256]{1,0:T(8,128)(2,1)}, u32[]{:S(2)}, u32[]{:S(2)}) collective-permute-start(bf16[8192,256]{1,0:T(8,128)(2,1)} %broadcast_select_fusion), channel_id=1, source_target_pairs={{8,16},{16,8},{9,17},{17,9},{10,18},{18,10},{11,19},{19,11},{12,20... | collective-permute-start | bytes 12582920 | tf_op jit(solution)/shard_map/ppermute | solution.py:78
  123.5 91.8 %all-to-all-start.2 = ((bf16[8,128,1024]{2,1,0:T(8,128)(2,1)}), bf16[8,128,1024]{2,1,0:T(8,128)(2,1)}, u32[]{:S(2)}, u32[]{:S(2)}) async-start(bf16[8,128,1024]{2,1,0:T(8,128)(2,1)} %bitcast.165), calls=%async_computation.2 | async-start | bytes 4194304 | tf_op jit(solution)/shard_map/all_to_all | solution.py:106
  218.4 288.2 %all-to-all-start.3 = ((bf16[8,128,1024]{2,1,0:T(8,128)(2,1)}), bf16[8,128,1024]{2,1,0:T(8,128)(2,1)}, u32[]{:S(2)}, u32[]{:S(2)}) async-start(bf16[8,128,1024]{2,1,0:T(8,128)(2,1)} %bitcast.166), calls=%async_computation.3 | async-start | bytes 4194304 | tf_op jit(solution)/shard_map/all_to_all | solution.py:106
  222.8 567.7 %reduce-scatter.9.cloned.1.call-start = ((), (), s32[]{:S(2)}) async-start(), calls=%async_computation.13 | async-start | bytes 1179648 | tf_op jit(solution)/shard_map/reduce_scatter | solution.py:181
  225.9 120.6 %collective-permute-start.9 = (bf16[8,128,1024]{2,1,0:T(8,128)(2,1)}, bf16[8,128,1024]{2,1,0:T(8,128)(2,1)S(1)}, u32[]{:S(2)}, u32[]{:S(2)}) collective-permute-start(bf16[8,128,1024]{2,1,0:T(8,128)(2,1)} %collective-permute-done.5), channel_id=1, source_target_pairs={{8,0},{9,1},{10,2},{11,3},{12,4},{13,5},{14,6},{15,7}} | collective-permute-start | bytes 6291464 | tf_op jit(solution)/shard_map/ppermute | solution.py:54
  231.7 118.2 %collective-permute-start.10 = (bf16[8,128,1024]{2,1,0:T(8,128)(2,1)}, bf16[8,128,1024]{2,1,0:T(8,128)(2,1)S(1)}, u32[]{:S(2)}, u32[]{:S(2)}) collective-permute-start(bf16[8,128,1024]{2,1,0:T(8,128)(2,1)} %collective-permute-done.6), channel_id=1, source_target_pairs={{16,24},{17,25},{18,26},{19,27},{20,28},{21,29},{22,30},{23,31}} | collective-permute-start | bytes 6291464 | tf_op jit(solution)/shard_map/ppermute | solution.py:49
  253.8 138.8 %collective-permute-start.11 = (bf16[8,128,1024]{2,1,0:T(8,128)(2,1)}, bf16[8,128,1024]{2,1,0:T(8,128)(2,1)S(1)}, u32[]{:S(2)}, u32[]{:S(2)}) collective-permute-start(bf16[8,128,1024]{2,1,0:T(8,128)(2,1)} %collective-permute-done.7), channel_id=1, source_target_pairs={{8,0},{9,1},{10,2},{11,3},{12,4},{13,5},{14,6},{15,7}} | collective-permute-start | bytes 6291464 | tf_op jit(solution)/shard_map/ppermute | solution.py:54
  264.1 217.3 %collective-permute-start.26 = (bf16[8192,256]{1,0:T(8,128)(2,1)}, bf16[8192,256]{1,0:T(8,128)(2,1)}, u32[]{:S(2)}, u32[]{:S(2)}) collective-permute-start(bf16[8192,256]{1,0:T(8,128)(2,1)} %broadcast_select_fusion.1), channel_id=1, source_target_pairs={{16,24},{8,0},{17,25},{9,1},{18,26},{10,2},{19,27},{11,3},{20,28},... | collective-permute-start | bytes 12582920 | tf_op jit(solution)/shard_map/ppermute | solution.py:78
  502.4 295.4 %reduce-scatter.11.cloned.1.call-start = ((), (), s32[]{:S(2)}) async-start(), calls=%async_computation.14 | async-start | bytes 1179648 | tf_op jit(solution)/shard_map/reduce_scatter | solution.py:181
  510.6 293.6 %reduce-scatter.13.cloned.1.call-start = ((), (), s32[]{:S(2)}) async-start(), calls=%async_computation.15 | async-start | bytes 1179648 | tf_op jit(solution)/shard_map/reduce_scatter | solution.py:181
  510.6 82.7 %collective-permute-start.14 = (bf16[8,128,1024]{2,1,0:T(8,128)(2,1)}, bf16[8,128,1024]{2,1,0:T(8,128)(2,1)}, u32[]{:S(2)}, u32[]{:S(2)}) collective-permute-start(bf16[8,128,1024]{2,1,0:T(8,128)(2,1)} %all-to-all-done.3), channel_id=1, source_target_pairs={{0,8},{8,16},{16,24},{1,9},{9,17},{17,25},{2,10},{10,18},{18,26},{... | collective-permute-start | bytes 6291464 | tf_op jit(solution)/shard_map/ppermute | solution.py:49
  516.5 84.4 %collective-permute-start.15 = (bf16[8,128,1024]{2,1,0:T(8,128)(2,1)}, bf16[8,128,1024]{2,1,0:T(8,128)(2,1)S(1)}, u32[]{:S(2)}, u32[]{:S(2)}) collective-permute-start(bf16[8,128,1024]{2,1,0:T(8,128)(2,1)} %all-to-all-done.3), channel_id=1, source_target_pairs={{8,0},{16,8},{24,16},{9,1},{17,9},{25,17},{10,2},{18,10},{26,18},{... | collective-permute-start | bytes 6291464 | tf_op jit(solution)/shard_map/ppermute | solution.py:54
  562.3 248.2 %reduce-scatter.15.cloned.1.call-start = ((), (), s32[]{:S(2)}) async-start(), calls=%async_computation.16 | async-start | bytes 1179648 | tf_op jit(solution)/shard_map/reduce_scatter | solution.py:181
  605.5 211.3 %reduce-scatter.17.cloned.1.call-start = ((), (), s32[]{:S(2)}) async-start(), calls=%async_computation.17 | async-start | bytes 1179648 | tf_op jit(solution)/shard_map/reduce_scatter | solution.py:181
  607.6 83.3 %collective-permute-start.19 = (bf16[8,128,1024]{2,1,0:T(8,128)(2,1)S(1)}, bf16[8,128,1024]{2,1,0:T(8,128)(2,1)}, u32[]{:S(2)}, u32[]{:S(2)}) collective-permute-start(bf16[8,128,1024]{2,1,0:T(8,128)(2,1)S(1)} %collective-permute-done.15), channel_id=1, source_target_pairs={{8,0},{16,8},{9,1},{17,9},{10,2},{18,10},{11,3},{19,11},{12,4},{20... | collective-permute-start | bytes 6291464 | tf_op jit(solution)/shard_map/ppermute | solution.py:54
  652.7 170.5 %reduce-scatter.19.cloned.1.call-start = ((), (), s32[]{:S(2)}) async-start(), calls=%async_computation.18 | async-start | bytes 1179648 | tf_op jit(solution)/shard_map/reduce_scatter | solution.py:181
  697.6 131.9 %reduce-scatter.21.cloned.1.call-start = ((), (), s32[]{:S(2)}) async-start(), calls=%async_computation.19 | async-start | bytes 1179648 | tf_op jit(solution)/shard_map/reduce_scatter | solution.py:181
  743.2 92.6 %reduce-scatter.23.cloned.1.call-start = ((), (), s32[]{:S(2)}) async-start(), calls=%async_computation.20 | async-start | bytes 1179648 | tf_op jit(solution)/shard_map/reduce_scatter | solution.py:181
  (22 other events, 978.9 us)
Sparse Core Ops, SparseCore 0:
  9.9 94.3 all-gather.1
  502.6 34.1 reduce-scatter.8
  540.0 35.9 reduce-scatter.10
  579.0 36.0 reduce-scatter.12
  618.1 36.0 reduce-scatter.14
  657.2 35.9 reduce-scatter.16
  697.7 34.6 reduce-scatter.18
  743.3 34.1 reduce-scatter.20
  786.0 33.9 reduce-scatter.22

commit v2 on v1

--- a/solution.py
+++ b/solution.py
@@ -100,53 +100,69 @@
     home_place = chosen % group
     my_place = my_rank % group
 
-    def by_rank(matrix, cut):
-        rows = matrix[cut * tall:(cut + 1) * tall].reshape(tall, ranks, width)
-        rows = jnp.transpose(rows, (1, 0, 2))
+    def across(rows):
+        rows = jnp.transpose(rows.reshape(tall, ranks, width), (1, 0, 2))
         return lax.all_to_all(rows, "tp", split_axis=0, concat_axis=0, tiled=True)
 
-    def put(whole, block, origin, cut):
-        return lax.dynamic_update_slice(whole, block[None, :, None], (origin, 0, cut, 0, 0))
-
+    def rows_of(matrix, cut):
+        return matrix[cut * tall:(cut + 1) * tall]
+
+    mine = {("q", 0): rows_of(query_weight, 0)}
+    last = ()
+    for name, matrix, cut in [("q", query_weight, 1), ("o", output_weight, 0), ("o", output_weight, 1)]:
+        mine[name, cut] = across(rows_of(after(matrix, *last) if last else matrix, cut))
+        last = (mine[name, cut],)
+    piece = lax.all_gather(after(tokens, mine["q", 1]), "tp", axis=1, tiled=True)
+
+    arrived = {}
+
+    def advance(name, cut, step, *earlier):
+        chain = arrived.setdefault((name, cut), {})
+        right = chain[step - 1, 0] if step > 1 else mine[name, cut]
+        left = chain[step - 1, 1] if step > 1 else mine[name, cut]
+        if earlier:
+            right, left = lax.optimization_barrier((right, left, *earlier))[:2]
+        chain[step, 0] = step_right(right, step)
+        chain[step, 1] = step_left(left, step)
+
+    def landed(name, cut, step):
+        return arrived[name, cut][step, 0], arrived[name, cut][step, 1]
+
+    final = replicas - 1
+    for step in range(1, replicas):
+        for cut in range(CUTS):
+            advance("q", cut, step)
     spread = keyval_spread(keyval_slot[0, 0], chosen // group)
+    for step in range(1, replicas):
+        for cut in range(CUTS):
+            wait = ()
+            if step == 1:
+                wait = (spread,) if cut else landed("q", CUTS - 1, final)
+            advance("o", cut, step, *wait)
     for level in range(group.bit_length() - 1):
         partner = partner_2(spread, "tp", level)
         holding = (my_place ^ home_place) >> level == 0
         spread = jnp.where(holding, spread, partner)
-    piece = lax.all_gather(tokens, "tp", axis=1, tiled=True)
-
-    mine = {}
-    last = None
-    for name, matrix in (("q", query_weight), ("o", output_weight)):
-        for cut in range(CUTS):
-            mine[name, cut] = by_rank(matrix if last is None else after(matrix, last), cut)
-            last = mine[name, cut]
-    arrived = {}
-    order = [(name, step, cut) for name in "qo" for step in range(1, replicas) for cut in range(CUTS)]
-    gate = []
-    for name, step, cut in order:
-        chain = arrived.setdefault((name, cut), {})
-        right = chain[step - 1, 0] if step > 1 else mine[name, cut]
-        left = chain[step - 1, 1] if step > 1 else mine[name, cut]
-        if len(gate) >= 2 * CUTS:
-            early = gate[-2 * CUTS]
-            if step == 1:
-                right, left = lax.optimization_barrier((right, left, *early))[:2]
-        chain[step, 0] = step_right(right, step)
-        chain[step, 1] = step_left(left, step)
-        gate.append((chain[step, 0], chain[step, 1]))
+    piece = after(piece, *landed("o", 0, max(final - 1, 1)))
+
+    def put(whole, block, origin, cut):
+        return lax.dynamic_update_slice(whole, block[None, :, None], (origin, 0, cut, 0, 0))
 
     def assemble(name):
         whole = jnp.zeros((replicas, ranks, CUTS, tall, width), jnp.bfloat16)
         parts = []
-        for cut in range(CUTS):
-            whole = put(whole, mine[name, cut], here, cut)
-            parts.append((mine[name, cut], here, cut))
-        for slot in slots:
+        for slot in [None] + slots:
+            blocks = []
             for cut in range(CUTS):
-                block, origin = slot_block(arrived[name, cut], slot)
+                if slot is None:
+                    block, origin = mine[name, cut], here
+                else:
+                    block, origin = slot_block(arrived[name, cut], slot)
+                if (name, cut) == ("q", 0):
+                    block = across(block)
                 whole = put(whole, block, origin, cut)
-                parts.append((block, origin, cut))
+                blocks.append(block)
+            parts.append((blocks, origin))
         return whole.reshape(-1, width), parts
 
     query_local, _ = assemble("q")
@@ -172,21 +188,33 @@
     context = context.astype(jnp.bfloat16).reshape(token_count, width)
 
     share = token_count // ranks
-    attended = jnp.zeros((share, replicas, ranks, CUTS, tall), jnp.bfloat16)
-    for block, origin, cut in output_parts:
-        partial = lax.dot_general(
+    attended = jnp.zeros((share, full), jnp.bfloat16)
+    span = ranks * height
+
+    def project(block):
+        return lax.dot_general(
             context, block.reshape(-1, width), (((1,), (1,)), ((), ())),
             preferred_element_type=jnp.float32,
         ).astype(jnp.bfloat16)
-        summed = lax.psum_scatter(partial, "tp", scatter_dimension=0, tiled=True)
-        attended = lax.dynamic_update_slice(
-            attended, summed.reshape(share, 1, ranks, 1, tall), (0, origin, 0, cut, 0)
-        )
+
+    for position, (blocks, origin) in enumerate(output_parts):
+        if position < len(output_parts) - 1:
+            partial = project(jnp.stack(blocks, axis=1))
+            summed = lax.psum_scatter(partial, "tp", scatter_dimension=0, tiled=True)
+        else:
+            sums = []
+            for block in blocks:
+                terms = project(block).reshape(ranks, share, -1)
+                terms = lax.all_to_all(terms, "tp", split_axis=0, concat_axis=0, tiled=True)
+                total = jnp.sum(terms.astype(jnp.float32), axis=0).astype(jnp.bfloat16)
+                sums.append(total.reshape(share, ranks, tall))
+            summed = jnp.stack(sums, axis=2).reshape(share, span)
+        attended = lax.dynamic_update_slice(attended, summed, (0, origin * span))
     return (
         query_local,
         output_local,
         spread.reshape(1, spread.shape[0], spread.shape[1]),
-        attended.reshape(share, -1),
+        attended,
     )
 
 

time: 860 us -> 784 us (0.912)
  waiting for transfers between devices: 518 us -> 340 us
  local copies, waits for them, and re-layouts: 86.1 us -> 162 us
  starting transfers between devices: 69.3 us -> 137 us
  blocking collectives: 41.5 us -> 0 us
    ppermute x12, waiting for transfers between devices: 301 us -> 224 us  [step_left(): lax.ppermute(block, 'rep', [(i, i - 1) for i in range(1, count - step + 1)])]
    dynamic_update_slice x4 -> x11, local copies, waits for them, and re-layouts: 12.3 us -> 65.3 us  [put(): lax.dynamic_update_slice(whole, block[None, :, None], (origin, 0, cut, 0,...]
    ppermute x12, waiting for transfers between devices: 109 us -> 56.7 us  [step_right(): lax.ppermute(block, 'rep', [(i, i + 1) for i in range(step - 1, count - 1)])]
    all_to_all x1 -> x0, blocking collectives: 41.5 us -> none  [by_rank(): return lax.all_to_all(rows, 'tp', split_axis=0, concat_axis=0, tiled=True)]
    dynamic_update_slice x8 -> x4, local copies, waits for them, and re-layouts: 42.2 us -> 2.95 us  [per_device(): attended = lax.dynamic_update_slice(attended, summed, (0, origin * span))]
    all_to_all x3 -> x9, starting transfers between devices: 13.2 us -> 52.2 us  [the longest x7 29.2 us: across(): return lax.all_to_all(rows, 'tp', split_axis=0, concat_axis=0, tiled=True)]
    ppermute x3, waiting for transfers between devices: 67.7 us -> 29.2 us  [keyval_spread(): got = lax.ppermute(old, 'rep', route)]
    ppermute x12, starting transfers between devices: 28.6 us -> 58.1 us  [step_right(): lax.ppermute(block, 'rep', [(i, i + 1) for i in range(step - 1, count - 1)])]
  transfers between devices with their start and end apart: 39 -> 40, of which waited for: 15 -> 17; matrix products, arithmetic and copies ran while one was open for 23% -> 35% of each run, Pallas kernels for 0% -> 0%
where the time goes in v2:
time: 784 us; the launch traced here: 773 us
  waiting for transfers between devices  340 us (43%)
  local copies, waits for them, and re-layouts  162 us (21%)
  starting transfers between devices  137 us (17%)
  other arithmetic  66.3 us (8%)
  matrix products  49 us (6%)
  between operations  18.6 us (2%)
    ppermute x12, waiting for transfers between devices, step_left(): lax.ppermute(block, 'rep', [(i, i - 1) for i in range(1, count - step + 1)])  224 us
    dynamic_update_slice x11, local copies, waits for them, and re-layouts, put(): lax.dynamic_update_slice(whole, block[None, :, None], (origin, 0, cut, 0,...  65.3 us
    ppermute x12, starting transfers between devices, step_right(): lax.ppermute(block, 'rep', [(i, i + 1) for i in range(step - 1, count - 1)])  58.1 us
    ppermute x12, waiting for transfers between devices, step_right(): lax.ppermute(block, 'rep', [(i, i + 1) for i in range(step - 1, count - 1)])  56.7 us
    all_to_all x7, waiting for transfers between devices, across(): return lax.all_to_all(rows, 'tp', split_axis=0, concat_axis=0, tiled=True)  30.1 us
    all_to_all x7, starting transfers between devices, across(): return lax.all_to_all(rows, 'tp', split_axis=0, concat_axis=0, tiled=True)  29.2 us
    ppermute x3, waiting for transfers between devices, keyval_spread(): got = lax.ppermute(old, 'rep', route)  29.2 us
    dynamic_update_slice x7, other arithmetic, put(): lax.dynamic_update_slice(whole, block[None, :, None], (origin, 0, cut, 0,...  24.5 us
  transfers between devices with their start and end apart: 40, of which 17 were waited for; matrix products, arithmetic and copies ran while one was open for 35% of the time, Pallas kernels for 0%

profile of v2, /device:TPU:0, one launch (start us, length us, event | category | flops | bytes accessed | tf_op | source)
XLA Modules:
  0.0 772.6 jit_solution(16720678189279063053)
XLA Ops:
  18.6 6.6 collective-permute-start.14
  31.4 31.0 %collective-permute-done = bf16[128,8192]{1,0:T(8,128)(2,1)} collective-permute-done((bf16[128,8192]{1,0:T(8,128)(2,1)}, bf16[128,8192]{1,0:T(8,128)(2,1)}, u32[]{:S(2)}, u32[]{:S(2)}) %collective-permute-start) | collective-permute-done | bytes 2097184 | tf_op jit(solution)/shard_map/ppermute | solution.py:49
  67.9 6.8 copy.74
  88.8 6.6 collective-permute-start.2
  97.4 20.0 %collective-permute-done.5 = bf16[128,8192]{1,0:T(8,128)(2,1)} collective-permute-done((bf16[128,8192]{1,0:T(8,128)(2,1)}, bf16[128,8192]{1,0:T(8,128)(2,1)}, u32[]{:S(2)}, u32[]{:S(2)}) %collective-permute-start.5) | collective-permute-done | bytes 2097184 | tf_op jit(solution)/shard_map/ppermute | solution.py:54
  123.0 29.2 %collective-permute-done.14 = bf16[8192,256]{1,0:T(8,128)(2,1)} collective-permute-done((bf16[8192,256]{1,0:T(8,128)(2,1)}, bf16[8192,256]{1,0:T(8,128)(2,1)}, u32[]{:S(2)}, u32[]{:S(2)}) %collective-permute-start.14) | collective-permute-done | bytes 4194336 | tf_op jit(solution)/shard_map/ppermute | solution.py:78
  170.3 25.7 %collective-permute-done.2 = bf16[8,128,1024]{1,2,0:T(8,128)(2,1)} collective-permute-done((bf16[8,128,1024]{1,2,0:T(8,128)(2,1)}, bf16[8,128,1024]{1,2,0:T(8,128)(2,1)}, u32[]{:S(2)}, u32[]{:S(2)}) %collective-permute-start.2) | collective-permute-done | bytes 2097184 | tf_op jit(solution)/shard_map/ppermute | solution.py:49
  216.8 12.2 %all-to-all-done.6 = bf16[8,128,1024]{1,2,0:T(8,128)(2,1)} async-done(((bf16[8,128,1024]{1,2,0:T(8,128)(2,1)}), bf16[8,128,1024]{1,2,0:T(8,128)(2,1)}, u32[]{:S(2)}, u32[]{:S(2)}) %all-to-all-start.6) | async-done | bytes 2097184 | tf_op jit(solution)/shard_map/all_to_all | solution.py:105
  234.7 15.3 %collective-permute-done.7 = bf16[8,128,1024]{1,2,0:T(8,128)(2,1)} collective-permute-done((bf16[8,128,1024]{1,2,0:T(8,128)(2,1)}, bf16[8,128,1024]{1,2,0:T(8,128)(2,1)}, u32[]{:S(2)}, u32[]{:S(2)}) %collective-permute-start.7) | collective-permute-done | bytes 2097184 | tf_op jit(solution)/shard_map/ppermute | solution.py:54
  275.8 15.2 %all-to-all-done.3 = bf16[8,128,1024]{1,2,0:T(8,128)(2,1)} async-done(((bf16[8,128,1024]{1,2,0:T(8,128)(2,1)}), bf16[8,128,1024]{1,2,0:T(8,128)(2,1)}, u32[]{:S(2)}, u32[]{:S(2)}) %all-to-all-start.3) | async-done | bytes 2097184 | tf_op jit(solution)/shard_map/all_to_all | solution.py:105
  316.7 30.9 %collective-permute-done.11 = bf16[8,128,1024]{1,2,0:T(8,128)(2,1)} collective-permute-done((bf16[8,128,1024]{1,2,0:T(8,128)(2,1)}, bf16[8,128,1024]{1,2,0:T(8,128)(2,1)}, u32[]{:S(2)}, u32[]{:S(2)}) %collective-permute-start.11) | collective-permute-done | bytes 2097184 | tf_op jit(solution)/shard_map/ppermute | solution.py:54
  348.9 21.2 %collective-permute-start.12 = (bf16[8,128,1024]{1,2,0:T(8,128)(2,1)}, bf16[8,128,1024]{1,2,0:T(8,128)(2,1)}, u32[]{:S(2)}, u32[]{:S(2)}) collective-permute-start(bf16[8,128,1024]{1,2,0:T(8,128)(2,1)} %copy-done), channel_id=1, source_target_pairs={{0,8},{8,16},{16,24},{1,9},{9,17},{17,25},{2,10},{10,18},{18,26},{... | collective-permute-start | bytes 6291464 | tf_op jit(solution)/shard_map/ppermute | solution.py:49
  379.7 21.8 %copy.69 = bf16[4,8,2,128,1024]{4,3,2,1,0:T(8,128)(2,1)} copy(bf16[4,8,2,128,1024]{3,4,1,2,0:T(8,128)(2,1)} %bitcast_dynamic-update-slice_fusion.8) | data formatting | bytes 33554432 | tf_op jit(solution)/shard_map/dynamic_update_slice | solution.py:149
  425.8 51.9 %collective-permute-done.13 = bf16[8,128,1024]{1,2,0:T(8,128)(2,1)S(1)} collective-permute-done((bf16[8,128,1024]{1,2,0:T(8,128)(2,1)}, bf16[8,128,1024]{1,2,0:T(8,128)(2,1)S(1)}, u32[]{:S(2)}, u32[]{:S(2)}) %collective-permute-start.13) | collective-permute-done | bytes 2097184 | tf_op jit(solution)/shard_map/ppermute | solution.py:54
  485.6 8.2 %collective-permute-start.17 = (bf16[8,128,1024]{1,2,0:T(8,128)(2,1)}, bf16[8,128,1024]{1,2,0:T(8,128)(2,1)}, u32[]{:S(2)}, u32[]{:S(2)}) collective-permute-start(bf16[8,128,1024]{1,2,0:T(8,128)(2,1)} %all-to-all-done.6), channel_id=1, source_target_pairs={{0,8},{8,16},{16,24},{1,9},{9,17},{17,25},{2,10},{10,18},{18,26},{... | collective-permute-start | bytes 6291464 | tf_op jit(solution)/shard_map/ppermute | solution.py:49
  495.1 33.2 %collective-permute-done.20 = bf16[8,128,1024]{1,2,0:T(8,128)(2,1)} collective-permute-done((bf16[8,128,1024]{1,2,0:T(8,128)(2,1)S(1)}, bf16[8,128,1024]{1,2,0:T(8,128)(2,1)}, u32[]{:S(2)}, u32[]{:S(2)}) %collective-permute-start.20) | collective-permute-done | bytes 2097184 | tf_op jit(solution)/shard_map/ppermute | solution.py:54
  528.3 7.0 convolution_convert_fusion.6
  535.3 12.6 %fusion.7 = bf16[64,8,8,128]{3,2,1,0:T(8,128)(2,1)S(1)} fusion(bf16[512,8192]{1,0:T(8,128)(2,1)S(1)} %copy-done.8, bf16[8192,1024]{1,0:T(8,128)(2,1)} %bitcast.127), kind=kOutput, calls=%fused_computation.46 | convolution fusion | flops 8590458880 | bytes 26214400 | tf_op jit(solution)/shard_map/dot_general | solution.py:172
  612.2 21.3 %collective-permute-done.22 = bf16[8,128,1024]{1,2,0:T(8,128)(2,1)} collective-permute-done((bf16[8,128,1024]{1,2,0:T(8,128)(2,1)}, bf16[8,128,1024]{1,2,0:T(8,128)(2,1)}, u32[]{:S(2)}, u32[]{:S(2)}) %collective-permute-start.22) | collective-permute-done | bytes 2097184 | tf_op jit(solution)/shard_map/ppermute | solution.py:54
  653.6 24.8 %collective-permute-done.24 = bf16[8,128,1024]{1,2,0:T(8,128)(2,1)} collective-permute-done((bf16[8,128,1024]{1,2,0:T(8,128)(2,1)}, bf16[8,128,1024]{1,2,0:T(8,128)(2,1)}, u32[]{:S(2)}, u32[]{:S(2)}) %collective-permute-start.24) | collective-permute-done | bytes 2097184 | tf_op jit(solution)/shard_map/ppermute | solution.py:54
  688.9 9.7 %all-to-all-start.7 = ((bf16[8,64,1024]{2,1,0:T(8,128)(2,1)}), bf16[8,64,1024]{2,1,0:T(8,128)(2,1)S(1)}, u32[]{:S(2)}, u32[]{:S(2)}) async-start(bf16[8,64,1024]{2,1,0:T(8,128)(2,1)} %bitcast.56), calls=%async_computation.10 | async-start | bytes 2097152 | tf_op jit(solution)/shard_map/all_to_all | solution.py:208
  698.6 16.2 %collective-permute-done.26 = bf16[8,128,1024]{1,2,0:T(8,128)(2,1)} collective-permute-done((bf16[8,128,1024]{1,2,0:T(8,128)(2,1)}, bf16[8,128,1024]{1,2,0:T(8,128)(2,1)}, u32[]{:S(2)}, u32[]{:S(2)}) %collective-permute-start.26) | collective-permute-done | bytes 2097184 | tf_op jit(solution)/shard_map/ppermute | solution.py:54
  725.5 13.2 %all-to-all-start.8 = ((bf16[8,64,1024]{2,1,0:T(8,128)(2,1)}), bf16[8,64,1024]{2,1,0:T(8,128)(2,1)S(1)}, u32[]{:S(2)}, u32[]{:S(2)}) async-start(bf16[8,64,1024]{2,1,0:T(8,128)(2,1)} %bitcast.58), calls=%async_computation.11 | async-start | bytes 2097152 | tf_op jit(solution)/shard_map/all_to_all | solution.py:208
  739.0 21.8 %copy.76 = bf16[4,8,2,128,1024]{4,3,2,1,0:T(8,128)(2,1)} copy(bf16[4,8,2,128,1024]{3,4,1,2,0:T(8,128)(2,1)} %get-tuple-element.20) | data formatting | bytes 33554432 | tf_op jit(solution)/shard_map/dynamic_update_slice | solution.py:149
  (154 shorter events, 291.7 us)
Async XLA Ops:
  18.6 133.6 %collective-permute-start.14 = (bf16[8192,256]{1,0:T(8,128)(2,1)}, bf16[8192,256]{1,0:T(8,128)(2,1)}, u32[]{:S(2)}, u32[]{:S(2)}) collective-permute-start(bf16[8192,256]{1,0:T(8,128)(2,1)} %bitcast.32), channel_id=1, source_target_pairs={{0,8},{24,16},{1,9},{25,17},{2,10},{26,18},{3,11},{27,19},{4,12},{... | collective-permute-start | bytes 12582920 | tf_op jit(solution)/shard_map/ppermute | solution.py:78
  81.4 446.8 %all-gather.2.cloned.1.call-start = ((), (), s32[]{:S(2)}) async-start(), calls=%async_computation.12 | async-start | bytes 9437184 | tf_op jit(solution)/shard_map/all_gather | solution.py:115
  87.5 81.5 %collective-permute-start.3 = (bf16[8,128,1024]{1,2,0:T(8,128)(2,1)}, bf16[8,128,1024]{1,2,0:T(8,128)(2,1)}, u32[]{:S(2)}, u32[]{:S(2)}) collective-permute-start(bf16[8,128,1024]{1,2,0:T(8,128)(2,1)} %copy-done.2), channel_id=1, source_target_pairs={{8,0},{16,8},{24,16},{9,1},{17,9},{25,17},{10,2},{18,10},{26,18},{... | collective-permute-start | bytes 6291464 | tf_op jit(solution)/shard_map/ppermute | solution.py:54
  88.8 107.2 %collective-permute-start.2 = (bf16[8,128,1024]{1,2,0:T(8,128)(2,1)}, bf16[8,128,1024]{1,2,0:T(8,128)(2,1)}, u32[]{:S(2)}, u32[]{:S(2)}) collective-permute-start(bf16[8,128,1024]{1,2,0:T(8,128)(2,1)} %copy-done.2), channel_id=1, source_target_pairs={{0,8},{8,16},{16,24},{1,9},{9,17},{17,25},{2,10},{10,18},{18,26},{... | collective-permute-start | bytes 6291464 | tf_op jit(solution)/shard_map/ppermute | solution.py:49
  95.4 107.0 %collective-permute-start.8 = (bf16[128,8192]{1,0:T(8,128)(2,1)}, bf16[128,8192]{1,0:T(8,128)(2,1)}, u32[]{:S(2)}, u32[]{:S(2)}) collective-permute-start(bf16[128,8192]{1,0:T(8,128)(2,1)} %collective-permute-done.4), channel_id=1, source_target_pairs={{16,24},{17,25},{18,26},{19,27},{20,28},{21,29},{22,30},{23,31}} | collective-permute-start | bytes 6291464 | tf_op jit(solution)/shard_map/ppermute | solution.py:49
  117.3 89.9 %collective-permute-start.9 = (bf16[128,8192]{1,0:T(8,128)(2,1)}, bf16[128,8192]{1,0:T(8,128)(2,1)}, u32[]{:S(2)}, u32[]{:S(2)}) collective-permute-start(bf16[128,8192]{1,0:T(8,128)(2,1)} %collective-permute-done.5), channel_id=1, source_target_pairs={{8,0},{9,1},{10,2},{11,3},{12,4},{13,5},{14,6},{15,7}} | collective-permute-start | bytes 6291464 | tf_op jit(solution)/shard_map/ppermute | solution.py:54
  118.7 79.3 %all-to-all-start = ((bf16[8,128,1024]{1,2,0:T(8,128)(2,1)}), bf16[8,128,1024]{1,2,0:T(8,128)(2,1)}, u32[]{:S(2)}, u32[]{:S(2)}) async-start(bf16[8,128,1024]{1,2,0:T(8,128)(2,1)} %bitcast.129), calls=%async_computation | async-start | bytes 4194304 | tf_op jit(solution)/shard_map/all_to_all | solution.py:105
  156.8 107.5 %collective-permute-start.15 = (bf16[8192,256]{1,0:T(8,128)(2,1)}, bf16[8192,256]{1,0:T(8,128)(2,1)}, u32[]{:S(2)}, u32[]{:S(2)}) collective-permute-start(bf16[8192,256]{1,0:T(8,128)(2,1)} %broadcast_select_fusion), channel_id=1, source_target_pairs={{8,16},{16,8},{9,17},{17,9},{10,18},{18,10},{11,19},{19,11},{12,20... | collective-permute-start | bytes 12582920 | tf_op jit(solution)/shard_map/ppermute | solution.py:78
  169.0 81.0 %collective-permute-start.7 = (bf16[8,128,1024]{1,2,0:T(8,128)(2,1)}, bf16[8,128,1024]{1,2,0:T(8,128)(2,1)}, u32[]{:S(2)}, u32[]{:S(2)}) collective-permute-start(bf16[8,128,1024]{1,2,0:T(8,128)(2,1)} %collective-permute-done.3), channel_id=1, source_target_pairs={{8,0},{16,8},{9,1},{17,9},{10,2},{18,10},{11,3},{19,11},{12,4},{20... | collective-permute-start | bytes 6291464 | tf_op jit(solution)/shard_map/ppermute | solution.py:54
  250.0 97.6 %collective-permute-start.11 = (bf16[8,128,1024]{1,2,0:T(8,128)(2,1)}, bf16[8,128,1024]{1,2,0:T(8,128)(2,1)}, u32[]{:S(2)}, u32[]{:S(2)}) collective-permute-start(bf16[8,128,1024]{1,2,0:T(8,128)(2,1)} %collective-permute-done.7), channel_id=1, source_target_pairs={{8,0},{9,1},{10,2},{11,3},{12,4},{13,5},{14,6},{15,7}} | collective-permute-start | bytes 6291464 | tf_op jit(solution)/shard_map/ppermute | solution.py:54
  251.3 96.3 %collective-permute-start.10 = (bf16[8,128,1024]{1,2,0:T(8,128)(2,1)}, bf16[8,128,1024]{1,2,0:T(8,128)(2,1)}, u32[]{:S(2)}, u32[]{:S(2)}) collective-permute-start(bf16[8,128,1024]{1,2,0:T(8,128)(2,1)} %collective-permute-done.6), channel_id=1, source_target_pairs={{16,24},{17,25},{18,26},{19,27},{20,28},{21,29},{22,30},{23,31}} | collective-permute-start | bytes 6291464 | tf_op jit(solution)/shard_map/ppermute | solution.py:49
  269.0 211.9 %collective-permute-start.16 = (bf16[8192,256]{1,0:T(8,128)(2,1)}, bf16[8192,256]{1,0:T(8,128)(2,1)}, u32[]{:S(2)}, u32[]{:S(2)}) collective-permute-start(bf16[8192,256]{1,0:T(8,128)(2,1)} %broadcast_select_fusion.1), channel_id=1, source_target_pairs={{16,24},{8,0},{17,25},{9,1},{18,26},{10,2},{19,27},{11,3},{20,28},... | collective-permute-start | bytes 12582920 | tf_op jit(solution)/shard_map/ppermute | solution.py:78
  291.0 110.5 %all-to-all-start.4 = ((bf16[8,128,1024]{1,2,0:T(8,128)(2,1)}), bf16[8,128,1024]{1,2,0:T(8,128)(2,1)}, u32[]{:S(2)}, u32[]{:S(2)}) async-start(bf16[8,128,1024]{1,2,0:T(8,128)(2,1)} %bitcast.132), calls=%async_computation.4 | async-start | bytes 4194304 | tf_op jit(solution)/shard_map/all_to_all | solution.py:105
  295.4 465.4 %reduce-scatter.4.cloned.1.call-start = ((), (), s32[]{:S(2)}) async-start(), calls=%async_computation.13 | async-start | bytes 2359296 | tf_op jit(solution)/shard_map/reduce_scatter | solution.py:203
  347.6 130.1 %collective-permute-start.13 = (bf16[8,128,1024]{1,2,0:T(8,128)(2,1)}, bf16[8,128,1024]{1,2,0:T(8,128)(2,1)S(1)}, u32[]{:S(2)}, u32[]{:S(2)}) collective-permute-start(bf16[8,128,1024]{1,2,0:T(8,128)(2,1)} %copy-done), channel_id=1, source_target_pairs={{8,0},{16,8},{24,16},{9,1},{17,9},{25,17},{10,2},{18,10},{26,18},{... | collective-permute-start | bytes 6291464 | tf_op jit(solution)/shard_map/ppermute | solution.py:54
  348.9 130.1 %collective-permute-start.12 = (bf16[8,128,1024]{1,2,0:T(8,128)(2,1)}, bf16[8,128,1024]{1,2,0:T(8,128)(2,1)}, u32[]{:S(2)}, u32[]{:S(2)}) collective-permute-start(bf16[8,128,1024]{1,2,0:T(8,128)(2,1)} %copy-done), channel_id=1, source_target_pairs={{0,8},{8,16},{16,24},{1,9},{9,17},{17,25},{2,10},{10,18},{18,26},{... | collective-permute-start | bytes 6291464 | tf_op jit(solution)/shard_map/ppermute | solution.py:49
  485.6 78.1 %collective-permute-start.17 = (bf16[8,128,1024]{1,2,0:T(8,128)(2,1)}, bf16[8,128,1024]{1,2,0:T(8,128)(2,1)}, u32[]{:S(2)}, u32[]{:S(2)}) collective-permute-start(bf16[8,128,1024]{1,2,0:T(8,128)(2,1)} %all-to-all-done.6), channel_id=1, source_target_pairs={{0,8},{8,16},{16,24},{1,9},{9,17},{17,25},{2,10},{10,18},{18,26},{... | collective-permute-start | bytes 6291464 | tf_op jit(solution)/shard_map/ppermute | solution.py:49
  493.8 73.0 %collective-permute-start.18 = (bf16[8,128,1024]{1,2,0:T(8,128)(2,1)}, bf16[8,128,1024]{1,2,0:T(8,128)(2,1)}, u32[]{:S(2)}, u32[]{:S(2)}) collective-permute-start(bf16[8,128,1024]{1,2,0:T(8,128)(2,1)} %all-to-all-done.6), channel_id=1, source_target_pairs={{8,0},{16,8},{24,16},{9,1},{17,9},{25,17},{10,2},{18,10},{26,18},{... | collective-permute-start | bytes 6291464 | tf_op jit(solution)/shard_map/ppermute | solution.py:54
  563.2 198.7 %reduce-scatter.6.cloned.1.call-start = ((), (), s32[]{:S(2)}) async-start(), calls=%async_computation.14 | async-start | bytes 2359296 | tf_op jit(solution)/shard_map/reduce_scatter | solution.py:203
  586.8 176.8 %reduce-scatter.8.cloned.1.call-start = ((), (), s32[]{:S(2)}) async-start(), calls=%async_computation.15 | async-start | bytes 2359296 | tf_op jit(solution)/shard_map/reduce_scatter | solution.py:203
  599.6 78.8 %collective-permute-start.24 = (bf16[8,128,1024]{1,2,0:T(8,128)(2,1)}, bf16[8,128,1024]{1,2,0:T(8,128)(2,1)}, u32[]{:S(2)}, u32[]{:S(2)}) collective-permute-start(bf16[8,128,1024]{1,2,0:T(8,128)(2,1)} %collective-permute-done.20), channel_id=1, source_target_pairs={{8,0},{9,1},{10,2},{11,3},{12,4},{13,5},{14,6},{15,7}} | collective-permute-start | bytes 6291464 | tf_op jit(solution)/shard_map/ppermute | solution.py:54
  600.8 77.5 %collective-permute-start.23 = (bf16[8,128,1024]{1,2,0:T(8,128)(2,1)}, bf16[8,128,1024]{1,2,0:T(8,128)(2,1)}, u32[]{:S(2)}, u32[]{:S(2)}) collective-permute-start(bf16[8,128,1024]{1,2,0:T(8,128)(2,1)} %collective-permute-done.19), channel_id=1, source_target_pairs={{16,24},{17,25},{18,26},{19,27},{20,28},{21,29},{22,30},{23,31}} | collective-permute-start | bytes 6291464 | tf_op jit(solution)/shard_map/ppermute | solution.py:49
  610.2 88.4 %collective-permute-start.25 = (bf16[8,128,1024]{1,2,0:T(8,128)(2,1)}, bf16[8,128,1024]{1,2,0:T(8,128)(2,1)}, u32[]{:S(2)}, u32[]{:S(2)}) collective-permute-start(bf16[8,128,1024]{1,2,0:T(8,128)(2,1)} %collective-permute-done.21), channel_id=1, source_target_pairs={{16,24},{17,25},{18,26},{19,27},{20,28},{21,29},{22,30},{23,31}} | collective-permute-start | bytes 6291464 | tf_op jit(solution)/shard_map/ppermute | solution.py:49
  633.5 81.3 %collective-permute-start.26 = (bf16[8,128,1024]{1,2,0:T(8,128)(2,1)}, bf16[8,128,1024]{1,2,0:T(8,128)(2,1)}, u32[]{:S(2)}, u32[]{:S(2)}) collective-permute-start(bf16[8,128,1024]{1,2,0:T(8,128)(2,1)} %collective-permute-done.22), channel_id=1, source_target_pairs={{8,0},{9,1},{10,2},{11,3},{12,4},{13,5},{14,6},{15,7}} | collective-permute-start | bytes 6291464 | tf_op jit(solution)/shard_map/ppermute | solution.py:54
  (27 other events, 1026.3 us)
Sparse Core Ops, SparseCore 0:
  87.6 85.4 all-gather.1
  563.3 45.7 reduce-scatter.3
  612.8 41.2 reduce-scatter.5
  657.2 45.3 reduce-scatter.7

commit v3 on v2

--- a/solution.py
+++ b/solution.py
@@ -110,7 +110,7 @@
     mine = {("q", 0): rows_of(query_weight, 0)}
     last = ()
     for name, matrix, cut in [("q", query_weight, 1), ("o", output_weight, 0), ("o", output_weight, 1)]:
-        mine[name, cut] = across(rows_of(after(matrix, *last) if last else matrix, cut))
+        mine[name, cut] = across(after(rows_of(matrix, cut), *last))
         last = (mine[name, cut],)
     piece = lax.all_gather(after(tokens, mine["q", 1]), "tp", axis=1, tiled=True)
 
@@ -197,18 +197,14 @@
             preferred_element_type=jnp.float32,
         ).astype(jnp.bfloat16)
 
-    for position, (blocks, origin) in enumerate(output_parts):
-        if position < len(output_parts) - 1:
-            partial = project(jnp.stack(blocks, axis=1))
-            summed = lax.psum_scatter(partial, "tp", scatter_dimension=0, tiled=True)
-        else:
-            sums = []
-            for block in blocks:
-                terms = project(block).reshape(ranks, share, -1)
-                terms = lax.all_to_all(terms, "tp", split_axis=0, concat_axis=0, tiled=True)
-                total = jnp.sum(terms.astype(jnp.float32), axis=0).astype(jnp.bfloat16)
-                sums.append(total.reshape(share, ranks, tall))
-            summed = jnp.stack(sums, axis=2).reshape(share, span)
+    for blocks, origin in output_parts:
+        sums = []
+        for block in blocks:
+            terms = project(block).reshape(ranks, share, -1)
+            terms = lax.all_to_all(terms, "tp", split_axis=0, concat_axis=0, tiled=True)
+            total = jnp.sum(terms.astype(jnp.float32), axis=0).astype(jnp.bfloat16)
+            sums.append(total.reshape(share, ranks, tall))
+        summed = jnp.stack(sums, axis=2).reshape(share, span)
         attended = lax.dynamic_update_slice(attended, summed, (0, origin * span))
     return (
         query_local,

time: 784 us -> 865 us (1.10)
  waiting for transfers between devices: 340 us -> 518 us
  local copies, waits for them, and re-layouts: 162 us -> 65.4 us
  starting transfers between devices: 137 us -> 127 us
    ppermute x12, waiting for transfers between devices: 224 us -> 280 us  [step_left(): lax.ppermute(block, 'rep', [(i, i - 1) for i in range(1, count - step + 1)])]
    all_to_all x7, waiting for transfers between devices: 30.1 us -> 76.7 us  [across(): return lax.all_to_all(rows, 'tp', split_axis=0, concat_axis=0, tiled=True)]
    ppermute x3, waiting for transfers between devices: 29.2 us -> 73.4 us  [keyval_spread(): got = lax.ppermute(old, 'rep', route)]
    dynamic_update_slice x11 -> x7, local copies, waits for them, and re-layouts: 65.3 us -> 21.7 us  [put(): lax.dynamic_update_slice(whole, block[None, :, None], (origin, 0, cut, 0,...]
    all_to_all x2 -> x8, waiting for transfers between devices: 0.01 us -> 41.9 us  [per_device(): terms = lax.all_to_all(terms, 'tp', split_axis=0, concat_axis=0, tiled=True)]
    ppermute x12, starting transfers between devices: 58.1 us -> 34.4 us  [step_right(): lax.ppermute(block, 'rep', [(i, i + 1) for i in range(step - 1, count - 1)])]
    another operation x5 -> x2, local copies, waits for them, and re-layouts: 31.7 us -> 12.2 us  [the longest x3 19.4 us: per_device(): partial = project(jnp.stack(blocks, axis=1))]
    dynamic_update_slice x7 -> x9, other arithmetic: 24.5 us -> 41.2 us  [put(): lax.dynamic_update_slice(whole, block[None, :, None], (origin, 0, cut, 0,...]
  transfers between devices with their start and end apart: 40 -> 43, of which waited for: 17 -> 20; matrix products, arithmetic and copies ran while one was open for 35% -> 18% of each run, Pallas kernels for 0% -> 0%
where the time goes in v3:
time: 865 us; the launch traced here: 856 us
  waiting for transfers between devices  518 us (60%)
  starting transfers between devices  127 us (15%)
  other arithmetic  73.7 us (9%)
  local copies, waits for them, and re-layouts  65.4 us (8%)
  matrix products  52.5 us (6%)
  between operations  19.1 us (2%)
    ppermute x12, waiting for transfers between devices, step_left(): lax.ppermute(block, 'rep', [(i, i - 1) for i in range(1, count - step + 1)])  280 us
    all_to_all x7, waiting for transfers between devices, across(): return lax.all_to_all(rows, 'tp', split_axis=0, concat_axis=0, tiled=True)  76.7 us
    ppermute x3, waiting for transfers between devices, keyval_spread(): got = lax.ppermute(old, 'rep', route)  73.4 us
    ppermute x12, waiting for transfers between devices, step_right(): lax.ppermute(block, 'rep', [(i, i + 1) for i in range(step - 1, count - 1)])  45.7 us
    all_to_all x8, waiting for transfers between devices, per_device(): terms = lax.all_to_all(terms, 'tp', split_axis=0, concat_axis=0, tiled=True)  41.9 us
    dynamic_update_slice x9, other arithmetic, put(): lax.dynamic_update_slice(whole, block[None, :, None], (origin, 0, cut, 0,...  41.2 us
    all_to_all x8, starting transfers between devices, per_device(): terms = lax.all_to_all(terms, 'tp', split_axis=0, concat_axis=0, tiled=True)  35.4 us
    ppermute x12, starting transfers between devices, step_right(): lax.ppermute(block, 'rep', [(i, i + 1) for i in range(step - 1, count - 1)])  34.4 us
  transfers between devices with their start and end apart: 43, of which 20 were waited for; matrix products, arithmetic and copies ran while one was open for 18% of the time, Pallas kernels for 0%

profile of v3, /device:TPU:0, one launch (start us, length us, event | category | flops | bytes accessed | tf_op | source)
XLA Modules:
  0.0 855.7 jit_solution(11055097723575597189)
XLA Ops:
  7.2 6.9 collective-permute-start.14
  30.0 73.4 %collective-permute-done.14 = bf16[8192,256]{1,0:T(8,128)(2,1)} collective-permute-done((bf16[8192,256]{1,0:T(8,128)(2,1)}, bf16[8192,256]{1,0:T(8,128)(2,1)}, u32[]{:S(2)}, u32[]{:S(2)}) %collective-permute-start.14) | collective-permute-done | bytes 4194336 | tf_op jit(solution)/shard_map/ppermute | solution.py:78
  112.0 7.2 collective-permute-start.2
  119.2 29.1 %collective-permute-done = bf16[128,8192]{1,0:T(8,128)(2,1)} collective-permute-done((bf16[128,8192]{1,0:T(8,128)(2,1)}, bf16[128,8192]{1,0:T(8,128)(2,1)}, u32[]{:S(2)}, u32[]{:S(2)}) %collective-permute-start) | collective-permute-done | bytes 2097184 | tf_op jit(solution)/shard_map/ppermute | solution.py:49
  166.7 29.6 %all-to-all-done.5 = bf16[8,128,1024]{2,1,0:T(8,128)(2,1)} async-done(((bf16[8,128,1024]{2,1,0:T(8,128)(2,1)}), bf16[8,128,1024]{2,1,0:T(8,128)(2,1)}, u32[]{:S(2)}, u32[]{:S(2)}) %all-to-all-start.5) | async-done | bytes 2097184 | tf_op jit(solution)/shard_map/all_to_all | solution.py:105
  216.5 28.4 %all-to-all-done = bf16[8,128,1024]{2,1,0:T(8,128)(2,1)} async-done(((bf16[8,128,1024]{2,1,0:T(8,128)(2,1)}), bf16[8,128,1024]{2,1,0:T(8,128)(2,1)}, u32[]{:S(2)}, u32[]{:S(2)}) %all-to-all-start) | async-done | bytes 2097184 | tf_op jit(solution)/shard_map/all_to_all | solution.py:105
  249.2 96.3 %collective-permute-done.9 = bf16[128,8192]{1,0:T(8,128)(2,1)} collective-permute-done((bf16[128,8192]{1,0:T(8,128)(2,1)}, bf16[128,8192]{1,0:T(8,128)(2,1)}, u32[]{:S(2)}, u32[]{:S(2)}) %collective-permute-start.9) | collective-permute-done | bytes 2097184 | tf_op jit(solution)/shard_map/ppermute | solution.py:54
  364.4 18.7 %all-to-all-done.2 = bf16[8,128,1024]{2,1,0:T(8,128)(2,1)} async-done(((bf16[8,128,1024]{2,1,0:T(8,128)(2,1)}), bf16[8,128,1024]{2,1,0:T(8,128)(2,1)}, u32[]{:S(2)}, u32[]{:S(2)}) %all-to-all-start.2) | async-done | bytes 2097184 | tf_op jit(solution)/shard_map/all_to_all | solution.py:105
  387.5 6.1 broadcast.9.clone
  399.8 6.1 broadcast.9.clone.1
  419.1 56.3 %collective-permute-done.11 = bf16[8,128,1024]{2,1,0:T(8,128)(2,1)} collective-permute-done((bf16[8,128,1024]{2,1,0:T(8,128)(2,1)}, bf16[8,128,1024]{2,1,0:T(8,128)(2,1)}, u32[]{:S(2)}, u32[]{:S(2)}) %collective-permute-start.11) | collective-permute-done | bytes 2097184 | tf_op jit(solution)/shard_map/ppermute | solution.py:54
  499.3 26.8 %collective-permute-done.13 = bf16[8,128,1024]{2,1,0:T(8,128)(2,1)} collective-permute-done((bf16[8,128,1024]{2,1,0:T(8,128)(2,1)}, bf16[8,128,1024]{2,1,0:T(8,128)(2,1)}, u32[]{:S(2)}, u32[]{:S(2)}) %collective-permute-start.13) | collective-permute-done | bytes 2097184 | tf_op jit(solution)/shard_map/ppermute | solution.py:54
  546.6 16.4 %collective-permute-done.17 = bf16[8,128,1024]{2,1,0:T(8,128)(2,1)} collective-permute-done((bf16[8,128,1024]{2,1,0:T(8,128)(2,1)}, bf16[8,128,1024]{2,1,0:T(8,128)(2,1)}, u32[]{:S(2)}, u32[]{:S(2)}) %collective-permute-start.17) | collective-permute-done | bytes 2097184 | tf_op jit(solution)/shard_map/ppermute | solution.py:49
  563.0 8.1 collective-permute-done.18
  575.8 32.7 %collective-permute-done.20 = bf16[8,128,1024]{2,1,0:T(8,128)(2,1)} collective-permute-done((bf16[8,128,1024]{2,1,0:T(8,128)(2,1)}, bf16[8,128,1024]{2,1,0:T(8,128)(2,1)}, u32[]{:S(2)}, u32[]{:S(2)}) %collective-permute-start.20) | collective-permute-done | bytes 2097184 | tf_op jit(solution)/shard_map/ppermute | solution.py:54
  613.7 7.0 convolution_convert_fusion.9
  620.8 12.7 %fusion.7 = bf16[64,8,8,128]{3,2,1,0:T(8,128)(2,1)S(1)} fusion(bf16[512,8192]{1,0:T(8,128)(2,1)S(1)} %copy-done.4, bf16[8192,1024]{1,0:T(8,128)(2,1)} %bitcast.17), kind=kOutput, calls=%fused_computation.54 | convolution fusion | flops 8590458880 | bytes 26214400 | tf_op jit(solution)/shard_map/dot_general | solution.py:172
  647.2 6.1 all-to-all-start.11
  656.8 11.9 %all-to-all-done.11 = bf16[8,64,1024]{2,1,0:T(8,128)(2,1)S(1)} async-done(((bf16[8,64,1024]{2,1,0:T(8,128)(2,1)}), bf16[8,64,1024]{2,1,0:T(8,128)(2,1)S(1)}, u32[]{:S(2)}, u32[]{:S(2)}) %all-to-all-start.11) | async-done | bytes 1048608 | tf_op jit(solution)/shard_map/all_to_all | solution.py:204
  697.1 11.2 %all-to-all-done.10 = bf16[8,64,1024]{2,1,0:T(8,128)(2,1)} async-done(((bf16[8,64,1024]{2,1,0:T(8,128)(2,1)}), bf16[8,64,1024]{2,1,0:T(8,128)(2,1)}, u32[]{:S(2)}, u32[]{:S(2)}) %all-to-all-start.10) | async-done | bytes 1048608 | tf_op jit(solution)/shard_map/all_to_all | solution.py:204
  718.7 12.1 %collective-permute-done.22 = bf16[8,128,1024]{2,1,0:T(8,128)(2,1)} collective-permute-done((bf16[8,128,1024]{2,1,0:T(8,128)(2,1)}, bf16[8,128,1024]{2,1,0:T(8,128)(2,1)}, u32[]{:S(2)}, u32[]{:S(2)}) %collective-permute-start.22) | collective-permute-done | bytes 2097184 | tf_op jit(solution)/shard_map/ppermute | solution.py:54
  741.6 34.2 %collective-permute-done.24 = bf16[8,128,1024]{2,1,0:T(8,128)(2,1)} collective-permute-done((bf16[8,128,1024]{2,1,0:T(8,128)(2,1)}, bf16[8,128,1024]{2,1,0:T(8,128)(2,1)}, u32[]{:S(2)}, u32[]{:S(2)}) %collective-permute-start.24) | collective-permute-done | bytes 2097184 | tf_op jit(solution)/shard_map/ppermute | solution.py:54
  806.7 13.5 %collective-permute-done.26 = bf16[8,128,1024]{2,1,0:T(8,128)(2,1)} collective-permute-done((bf16[8,128,1024]{2,1,0:T(8,128)(2,1)}, bf16[8,128,1024]{2,1,0:T(8,128)(2,1)}, u32[]{:S(2)}, u32[]{:S(2)}) %collective-permute-start.26) | collective-permute-done | bytes 2097184 | tf_op jit(solution)/shard_map/ppermute | solution.py:54
  837.4 9.5 %all-to-all-done.14 = bf16[8,64,1024]{2,1,0:T(8,128)(2,1)S(1)} async-done(((bf16[8,64,1024]{2,1,0:T(8,128)(2,1)}), bf16[8,64,1024]{2,1,0:T(8,128)(2,1)S(1)}, u32[]{:S(2)}, u32[]{:S(2)}) %all-to-all-start.14) | async-done | bytes 1048608 | tf_op jit(solution)/shard_map/all_to_all | solution.py:204
  (160 shorter events, 276.2 us)
Async XLA Ops:
  7.2 96.2 %collective-permute-start.14 = (bf16[8192,256]{1,0:T(8,128)(2,1)}, bf16[8192,256]{1,0:T(8,128)(2,1)}, u32[]{:S(2)}, u32[]{:S(2)}) collective-permute-start(bf16[8192,256]{1,0:T(8,128)(2,1)} %bitcast.219), channel_id=1, source_target_pairs={{0,8},{24,16},{1,9},{25,17},{2,10},{26,18},{3,11},{27,19},{4,12},{... | collective-permute-start | bytes 12582920 | tf_op jit(solution)/shard_map/ppermute | solution.py:78
  18.0 130.3 %collective-permute-start = (bf16[128,8192]{1,0:T(8,128)(2,1)}, bf16[128,8192]{1,0:T(8,128)(2,1)}, u32[]{:S(2)}, u32[]{:S(2)}) collective-permute-start(bf16[128,8192]{1,0:T(8,128)(2,1)} %get-tuple-element.37), channel_id=1, source_target_pairs={{0,8},{8,16},{16,24},{1,9},{9,17},{17,25},{2,10},{10,18},{18,26},{... | collective-permute-start | bytes 6291464 | tf_op jit(solution)/shard_map/ppermute | solution.py:49
  20.7 129.6 %collective-permute-start.1 = (bf16[128,8192]{1,0:T(8,128)(2,1)}, bf16[128,8192]{1,0:T(8,128)(2,1)}, u32[]{:S(2)}, u32[]{:S(2)}) collective-permute-start(bf16[128,8192]{1,0:T(8,128)(2,1)} %get-tuple-element.37), channel_id=1, source_target_pairs={{8,0},{16,8},{24,16},{9,1},{17,9},{25,17},{10,2},{18,10},{26,18},{... | collective-permute-start | bytes 6291464 | tf_op jit(solution)/shard_map/ppermute | solution.py:54
  23.6 87.2 %all-to-all-start.1 = ((bf16[8,128,1024]{2,1,0:T(8,128)(2,1)}), bf16[8,128,1024]{2,1,0:T(8,128)(2,1)}, u32[]{:S(2)}, u32[]{:S(2)}) async-start(bf16[8,128,1024]{2,1,0:T(8,128)(2,1)} %bitcast.204), calls=%async_computation.1 | async-start | bytes 4194304 | tf_op jit(solution)/shard_map/all_to_all | solution.py:105
  108.0 102.5 %collective-permute-start.15 = (bf16[8192,256]{1,0:T(8,128)(2,1)}, bf16[8192,256]{1,0:T(8,128)(2,1)}, u32[]{:S(2)}, u32[]{:S(2)}) collective-permute-start(bf16[8192,256]{1,0:T(8,128)(2,1)} %broadcast_select_fusion), channel_id=1, source_target_pairs={{8,16},{16,8},{9,17},{17,9},{10,18},{18,10},{11,19},{19,11},{12,20... | collective-permute-start | bytes 12582920 | tf_op jit(solution)/shard_map/ppermute | solution.py:78
  110.7 93.2 %collective-permute-start.3 = (bf16[8,128,1024]{2,1,0:T(8,128)(2,1)}, bf16[8,128,1024]{2,1,0:T(8,128)(2,1)S(1)}, u32[]{:S(2)}, u32[]{:S(2)}) collective-permute-start(bf16[8,128,1024]{2,1,0:T(8,128)(2,1)} %all-to-all-done.1), channel_id=1, source_target_pairs={{8,0},{16,8},{24,16},{9,1},{17,9},{25,17},{10,2},{18,10},{26,18},{... | collective-permute-start | bytes 6291464 | tf_op jit(solution)/shard_map/ppermute | solution.py:54
  112.0 93.2 %collective-permute-start.2 = (bf16[8,128,1024]{2,1,0:T(8,128)(2,1)}, bf16[8,128,1024]{2,1,0:T(8,128)(2,1)}, u32[]{:S(2)}, u32[]{:S(2)}) collective-permute-start(bf16[8,128,1024]{2,1,0:T(8,128)(2,1)} %all-to-all-done.1), channel_id=1, source_target_pairs={{0,8},{8,16},{16,24},{1,9},{9,17},{17,25},{2,10},{10,18},{18,26},{... | collective-permute-start | bytes 6291464 | tf_op jit(solution)/shard_map/ppermute | solution.py:49
  161.5 452.2 %all-gather.2.cloned.1.call-start = ((), (), s32[]{:S(2)}) async-start(), calls=%async_computation.15 | async-start | bytes 9437184 | tf_op jit(solution)/shard_map/all_gather | solution.py:115
  203.9 153.9 %collective-permute-start.7 = (bf16[8,128,1024]{2,1,0:T(8,128)(2,1)S(1)}, bf16[8,128,1024]{2,1,0:T(8,128)(2,1)}, u32[]{:S(2)}, u32[]{:S(2)}) collective-permute-start(bf16[8,128,1024]{2,1,0:T(8,128)(2,1)S(1)} %collective-permute-done.3), channel_id=1, source_target_pairs={{8,0},{16,8},{9,1},{17,9},{10,2},{18,10},{11,3},{19,11},{12,4},{20... | collective-permute-start | bytes 6291464 | tf_op jit(solution)/shard_map/ppermute | solution.py:54
  205.2 153.9 %collective-permute-start.6 = (bf16[8,128,1024]{2,1,0:T(8,128)(2,1)}, bf16[8,128,1024]{2,1,0:T(8,128)(2,1)}, u32[]{:S(2)}, u32[]{:S(2)}) collective-permute-start(bf16[8,128,1024]{2,1,0:T(8,128)(2,1)} %collective-permute-done.2), channel_id=1, source_target_pairs={{8,16},{16,24},{9,17},{17,25},{10,18},{18,26},{11,19},{19,27},{12,... | collective-permute-start | bytes 6291464 | tf_op jit(solution)/shard_map/ppermute | solution.py:49
  209.2 136.3 %collective-permute-start.9 = (bf16[128,8192]{1,0:T(8,128)(2,1)}, bf16[128,8192]{1,0:T(8,128)(2,1)}, u32[]{:S(2)}, u32[]{:S(2)}) collective-permute-start(bf16[128,8192]{1,0:T(8,128)(2,1)} %collective-permute-done.5), channel_id=1, source_target_pairs={{8,0},{9,1},{10,2},{11,3},{12,4},{13,5},{14,6},{15,7}} | collective-permute-start | bytes 6291464 | tf_op jit(solution)/shard_map/ppermute | solution.py:54
  215.2 271.7 %collective-permute-start.16 = (bf16[8192,256]{1,0:T(8,128)(2,1)}, bf16[8192,256]{1,0:T(8,128)(2,1)}, u32[]{:S(2)}, u32[]{:S(2)}) collective-permute-start(bf16[8192,256]{1,0:T(8,128)(2,1)} %broadcast_select_fusion.1), channel_id=1, source_target_pairs={{16,24},{8,0},{17,25},{9,1},{18,26},{10,2},{19,27},{11,3},{20,28},... | collective-permute-start | bytes 12582920 | tf_op jit(solution)/shard_map/ppermute | solution.py:78
  244.8 107.2 %all-to-all-start.6 = ((bf16[8,128,1024]{2,1,0:T(8,128)(2,1)}), bf16[8,128,1024]{2,1,0:T(8,128)(2,1)}, u32[]{:S(2)}, u32[]{:S(2)}) async-start(bf16[8,128,1024]{2,1,0:T(8,128)(2,1)} %bitcast.211), calls=%async_computation.6 | async-start | bytes 4194304 | tf_op jit(solution)/shard_map/all_to_all | solution.py:105
  357.8 117.5 %collective-permute-start.11 = (bf16[8,128,1024]{2,1,0:T(8,128)(2,1)}, bf16[8,128,1024]{2,1,0:T(8,128)(2,1)}, u32[]{:S(2)}, u32[]{:S(2)}) collective-permute-start(bf16[8,128,1024]{2,1,0:T(8,128)(2,1)} %collective-permute-done.7), channel_id=1, source_target_pairs={{8,0},{9,1},{10,2},{11,3},{12,4},{13,5},{14,6},{15,7}} | collective-permute-start | bytes 6291464 | tf_op jit(solution)/shard_map/ppermute | solution.py:54
  359.1 116.2 %collective-permute-start.10 = (bf16[8,128,1024]{2,1,0:T(8,128)(2,1)}, bf16[8,128,1024]{2,1,0:T(8,128)(2,1)}, u32[]{:S(2)}, u32[]{:S(2)}) collective-permute-start(bf16[8,128,1024]{2,1,0:T(8,128)(2,1)} %collective-permute-done.6), channel_id=1, source_target_pairs={{16,24},{17,25},{18,26},{19,27},{20,28},{21,29},{22,30},{23,31}} | collective-permute-start | bytes 6291464 | tf_op jit(solution)/shard_map/ppermute | solution.py:49
  383.1 99.4 %all-to-all-start.3 = ((bf16[8,128,1024]{2,1,0:T(8,128)(2,1)}), bf16[8,128,1024]{2,1,0:T(8,128)(2,1)}, u32[]{:S(2)}, u32[]{:S(2)}) async-start(bf16[8,128,1024]{2,1,0:T(8,128)(2,1)} %bitcast.214), calls=%async_computation.3 | async-start | bytes 4194304 | tf_op jit(solution)/shard_map/all_to_all | solution.py:105
  491.6 71.4 %collective-permute-start.17 = (bf16[8,128,1024]{2,1,0:T(8,128)(2,1)}, bf16[8,128,1024]{2,1,0:T(8,128)(2,1)}, u32[]{:S(2)}, u32[]{:S(2)}) collective-permute-start(bf16[8,128,1024]{2,1,0:T(8,128)(2,1)} %all-to-all-done.6), channel_id=1, source_target_pairs={{0,8},{8,16},{16,24},{1,9},{9,17},{17,25},{2,10},{10,18},{18,26},{... | collective-permute-start | bytes 6291464 | tf_op jit(solution)/shard_map/ppermute | solution.py:49
  494.9 76.2 %collective-permute-start.18 = (bf16[8,128,1024]{2,1,0:T(8,128)(2,1)}, bf16[8,128,1024]{2,1,0:T(8,128)(2,1)}, u32[]{:S(2)}, u32[]{:S(2)}) collective-permute-start(bf16[8,128,1024]{2,1,0:T(8,128)(2,1)} %all-to-all-done.6), channel_id=1, source_target_pairs={{8,0},{16,8},{24,16},{9,1},{17,9},{25,17},{10,2},{18,10},{26,18},{... | collective-permute-start | bytes 6291464 | tf_op jit(solution)/shard_map/ppermute | solution.py:54
  526.1 82.4 %collective-permute-start.20 = (bf16[8,128,1024]{2,1,0:T(8,128)(2,1)}, bf16[8,128,1024]{2,1,0:T(8,128)(2,1)}, u32[]{:S(2)}, u32[]{:S(2)}) collective-permute-start(bf16[8,128,1024]{2,1,0:T(8,128)(2,1)} %collective-permute-done.13), channel_id=1, source_target_pairs={{8,0},{16,8},{9,1},{17,9},{10,2},{18,10},{11,3},{19,11},{12,4},{20... | collective-permute-start | bytes 6291464 | tf_op jit(solution)/shard_map/ppermute | solution.py:54
  527.6 80.9 %collective-permute-start.19 = (bf16[8,128,1024]{2,1,0:T(8,128)(2,1)}, bf16[8,128,1024]{2,1,0:T(8,128)(2,1)}, u32[]{:S(2)}, u32[]{:S(2)}) collective-permute-start(bf16[8,128,1024]{2,1,0:T(8,128)(2,1)} %collective-permute-done.12), channel_id=1, source_target_pairs={{8,16},{16,24},{9,17},{17,25},{10,18},{18,26},{11,19},{19,27},{12,... | collective-permute-start | bytes 6291464 | tf_op jit(solution)/shard_map/ppermute | solution.py:49
  675.1 100.7 %collective-permute-start.24 = (bf16[8,128,1024]{2,1,0:T(8,128)(2,1)}, bf16[8,128,1024]{2,1,0:T(8,128)(2,1)}, u32[]{:S(2)}, u32[]{:S(2)}) collective-permute-start(bf16[8,128,1024]{2,1,0:T(8,128)(2,1)} %collective-permute-done.20), channel_id=1, source_target_pairs={{8,0},{9,1},{10,2},{11,3},{12,4},{13,5},{14,6},{15,7}} | collective-permute-start | bytes 6291464 | tf_op jit(solution)/shard_map/ppermute | solution.py:54
  676.4 99.4 %collective-permute-start.23 = (bf16[8,128,1024]{2,1,0:T(8,128)(2,1)}, bf16[8,128,1024]{2,1,0:T(8,128)(2,1)}, u32[]{:S(2)}, u32[]{:S(2)}) collective-permute-start(bf16[8,128,1024]{2,1,0:T(8,128)(2,1)} %collective-permute-done.19), channel_id=1, source_target_pairs={{16,24},{17,25},{18,26},{19,27},{20,28},{21,29},{22,30},{23,31}} | collective-permute-start | bytes 6291464 | tf_op jit(solution)/shard_map/ppermute | solution.py:49
  716.8 90.0 %collective-permute-start.25 = (bf16[8,128,1024]{2,1,0:T(8,128)(2,1)S(1)}, bf16[8,128,1024]{2,1,0:T(8,128)(2,1)}, u32[]{:S(2)}, u32[]{:S(2)}) collective-permute-start(bf16[8,128,1024]{2,1,0:T(8,128)(2,1)S(1)} %collective-permute-done.21), channel_id=1, source_target_pairs={{16,24},{17,25},{18,26},{19,27},{20,28},{21,29},{22,30},{23,31}} | collective-permute-start | bytes 6291464 | tf_op jit(solution)/shard_map/ppermute | solution.py:49
  730.9 89.3 %collective-permute-start.26 = (bf16[8,128,1024]{2,1,0:T(8,128)(2,1)}, bf16[8,128,1024]{2,1,0:T(8,128)(2,1)}, u32[]{:S(2)}, u32[]{:S(2)}) collective-permute-start(bf16[8,128,1024]{2,1,0:T(8,128)(2,1)} %collective-permute-done.22), channel_id=1, source_target_pairs={{8,0},{9,1},{10,2},{11,3},{12,4},{13,5},{14,6},{15,7}} | collective-permute-start | bytes 6291464 | tf_op jit(solution)/shard_map/ppermute | solution.py:54
  (28 other events, 772.3 us)
Sparse Core Ops, SparseCore 0:
  164.2 86.8 all-gather.1
